TPU v7x, 256 devices: a whole 4x4x8 slice. The times are simulated.
256 devices in a mesh: pos: 16 (over z, core), ty: 4 (over x), tx: 4 (over y).
Axes of the slice: x: 4, y: 4, z: 8, core: 2. Of those that a mesh axis runs over, the one named last changes fastest.
Arguments:
- object_field: float32 [2, 1536, 1536], P(None, 'ty', 'tx'), may hold values from -5 to 5
- probe: float32 [4, 2, 256, 256], replicated, may hold values from -4 to 4
- amplitudes: float32 [512, 256, 256], P(('pos', 'ty', 'tx')), may hold values from 0.5 to 4
- live_pixels: int32 [256, 256], replicated, may hold values 0 or 1
- offsets: int32 [512, 2], P(('pos', 'ty', 'tx')), may hold values from 0 to 1280, as said below
Outputs:
- object_new: float32 [2, 1536, 1536], P(None, 'ty', 'tx')
- probe_new: float32 [4, 2, 256, 256], replicated
Inputs may be any that keep to these rules, and one draw needn't show every extreme that they name: The position of row b of offsets starts inside object tile (((b // 2) // 4) % 4, (b // 2) % 4) of 384 x 384 pixels, and its whole window lies inside the object.
All inputs are finite; a program needn't handle non-finite values.
Results may differ from a plain program's by a relative error of at most 0.0001.
Values sent between devices are 32-bit elements; how exact they have to be, the bound alone decides.
A program may use at most 64 MiB of HBM per device.

v0:
```python
import math

import jax
import jax.numpy as jnp
from jax import lax
from jax.sharding import PartitionSpec as P

intensity_floor = 0.25
flux_floor = 0.25
tv_weight = 0.1


def passed_along(x, axis, by):
    devices = lax.axis_size(axis)
    pairs = [(i, i + by) for i in range(devices) if 0 <= i + by < devices]
    return lax.ppermute(x, axis, pairs)


def padded_2(x, sides, width):
    for axis, dim in sides:
        devices, length = (lax.axis_size(axis), x.shape[dim])
        up = [(i, (i + 1) % devices) for i in range(devices - 1)]
        down = [(j, i) for i, j in up]
        last = lax.slice_in_dim(x, length - width, length, axis=dim)
        first = lax.slice_in_dim(x, 0, width, axis=dim)
        before = lax.ppermute(last, axis, up)
        after = lax.ppermute(first, axis, down)
        x = jnp.concatenate([before, x, after], axis=dim)
    return x


def left_product(table, field):
    return jnp.einsum("kn,mnl->mkl", table, field, precision=lax.Precision.HIGHEST)


def right_product(field, table):
    return jnp.einsum("mkn,nl->mkl", field, table, precision=lax.Precision.HIGHEST)


def transform(field_real, field_imag, cosine, sine, sign):
    half_real = left_product(cosine, field_real) - sign * left_product(sine, field_imag)
    half_imag = left_product(cosine, field_imag) + sign * left_product(sine, field_real)
    out_real = right_product(half_real, cosine) - sign * right_product(half_imag, sine)
    out_imag = right_product(half_imag, cosine) + sign * right_product(half_real, sine)
    return (out_real, out_imag)


def fold_rims(accum, tile):
    column_part = passed_along(accum[:, :, tile:], "tx", 1)
    folded = accum[:, :, :tile]
    folded = folded.at[:, :, : column_part.shape[2]].add(column_part)
    row_part = passed_along(folded[:, tile:, :], "ty", 1)
    result = folded[:, :tile, :]
    return result.at[:, : row_part.shape[1], :].add(row_part)


def body(object_field, probe, amplitudes, live_pixels, offsets):
    tile = object_field.shape[1]
    width = probe.shape[-1]
    slots = amplitudes.shape[0]
    right = passed_along(object_field[:, :, :width], "tx", -1)
    widened = jnp.concatenate([object_field, right], axis=2)
    lower = passed_along(widened[:, :width, :], "ty", -1)
    extended = jnp.concatenate([widened, lower], axis=1)
    row_base = lax.axis_index("ty") * tile
    col_base = lax.axis_index("tx") * tile
    indices = jnp.arange(width, dtype=jnp.int32)
    angles = (
        2.0 * math.pi / width * (indices[:, None] * indices[None, :] % width).astype(jnp.float32)
    )
    cosine = jnp.cos(angles) / math.sqrt(width)
    sine = jnp.sin(angles) / math.sqrt(width)
    probe_real = probe[:, 0]
    probe_imag = probe[:, 1]
    weight = jnp.sum(probe_real * probe_real + probe_imag * probe_imag, axis=0)
    live = live_pixels == 1
    zero_index = jnp.zeros((), jnp.int32)
    channels = 3

    def visit(slot_index, carry):
        accum, numer, denom = carry
        local_row = offsets[slot_index, 0] - row_base
        local_col = offsets[slot_index, 1] - col_base
        patch = lax.dynamic_slice(extended, (zero_index, local_row, local_col), (2, width, width))
        patch_real = patch[0]
        patch_imag = patch[1]
        wave_real = probe_real * patch_real - probe_imag * patch_imag
        wave_imag = probe_real * patch_imag + probe_imag * patch_real
        far_real, far_imag = transform(wave_real, wave_imag, cosine, sine, -1.0)
        intensity = jnp.sum(far_real * far_real + far_imag * far_imag, axis=0)
        factor = jnp.where(
            live, amplitudes[slot_index] / jnp.sqrt(jnp.maximum(intensity, intensity_floor)), 1.0
        )
        near_real, near_imag = transform(far_real * factor, far_imag * factor, cosine, sine, 1.0)
        delta_real = near_real - wave_real
        delta_imag = near_imag - wave_imag
        grad_real = jnp.sum(probe_real * delta_real + probe_imag * delta_imag, axis=0)
        grad_imag = jnp.sum(probe_real * delta_imag - probe_imag * delta_real, axis=0)
        terms = jnp.stack([grad_real, grad_imag, weight][:channels])
        region = lax.dynamic_slice(
            accum, (zero_index, local_row, local_col), (channels, width, width)
        )
        accum = lax.dynamic_update_slice(accum, region + terms, (zero_index, local_row, local_col))
        numer = numer + jnp.stack(
            [
                patch_real * delta_real + patch_imag * delta_imag,
                patch_real * delta_imag - patch_imag * delta_real,
            ],
            axis=1,
        )
        denom = denom + patch_real * patch_real + patch_imag * patch_imag
        return (accum, numer, denom)

    accum0 = jnp.zeros((channels, tile + width, tile + width), jnp.float32)
    numer0 = jnp.zeros_like(probe)
    denom0 = jnp.zeros((width, width), jnp.float32)
    accum, numer, denom = lax.fori_loop(0, slots, visit, (accum0, numer0, denom0))
    numer, denom = lax.psum((numer, denom), ("pos", "ty", "tx"))
    accum = lax.psum(accum, "pos")
    grads = fold_rims(accum, tile)
    weight_tile = grads[2]
    probe_new = probe + numer / (denom + 1.0)
    updated = object_field + grads[:2] / (weight_tile + 1.0)
    padded = padded_2(updated, (("ty", 1), ("tx", 2)), 1)
    base = padded[:, : tile + 1, : tile + 1]
    flux_x = padded[:, : tile + 1, 1 : tile + 2] - base
    flux_y = padded[:, 1 : tile + 2, : tile + 1] - base
    magnitude = jnp.sqrt(
        jnp.maximum(jnp.sum(flux_x * flux_x + flux_y * flux_y, axis=0), flux_floor)
    )
    norm_x = flux_x / magnitude
    norm_y = flux_y / magnitude
    divergence = norm_x[:, 1:, 1:] - norm_x[:, 1:, :-1] + norm_y[:, 1:, 1:] - norm_y[:, :-1, 1:]
    object_new = updated + tv_weight * divergence
    return (object_new, probe_new)


def solution(mesh):
    return jax.shard_map(
        body,
        mesh=mesh,
        in_specs=(
            P(None, "ty", "tx"),
            P(),
            P(("pos", "ty", "tx"), None, None),
            P(),
            P(("pos", "ty", "tx"), None),
        ),
        out_specs=(P(None, "ty", "tx"), P()),
        check_vma=False,
    )
```

profile of v0, /device:TPU:1, one launch (start us, length us, event | category | flops | bytes accessed | tf_op | source)
XLA Modules:
  0.0 672.1 jit_solution(15663612649759757686)
XLA Ops:
  10.7 17.6 %collective-permute-done = f32[2,384,256]{2,1,0:T(8,128)S(1)} collective-permute-done((f32[2,384,256]{2,1,0:T(8,128)S(1)}, f32[2,384,256]{2,1,0:T(8,128)S(1)}, u32[]{:S(2)}, u32[]{:S(2)}) %collective-permute-start) | collective-permute-done | bytes 786464 | tf_op jit(solution)/shard_map/ppermute | solution.py:16
  34.1 29.6 %collective-permute-done.1 = f32[2,256,640]{2,1,0:T(8,128)} collective-permute-done((f32[2,256,640]{2,1,0:T(8,128)}, f32[2,256,640]{2,1,0:T(8,128)}, u32[]{:S(2)}, u32[]{:S(2)}) %collective-permute-start.1) | collective-permute-done | bytes 1310752 | tf_op jit(solution)/shard_map/ppermute | solution.py:16
  63.7 3.2 pad_maximum_fusion
  69.4 129.8 %while.21 = (s32[]{:T(128)}, f32[3,640,640]{2,1,0:T(8,128)}, f32[4,2,256,256]{3,2,0,1:T(8,128)}, f32[256,256]{1,0:T(8,128)S(1)}, s32[2,2]{1,0:T(2,128)S(1)}, /*i...) while((s32[]{:T(128)}, f32[3,640,640]{2,1,0:T(8,128)}, ...), condition=%wide.region_5.6_spmd.clone.clone, body=%wide.region_1.5_spmd.clone.clone.sunk | while | flops 12914130944 | bytes 69009736 | solution.py:117
  83.9 3.2 fusion.237
  109.8 2.9 fusion.249
  115.4 3.3 add_bitcast_fusion.2
  122.1 8.9 %dynamic_update_slice.10 = f32[3,640,640]{2,1,0:T(8,128)} dynamic-update-slice(f32[3,640,640]{2,1,0:T(8,128)} %get-tuple-element.586, f32[3,256,256]{2,1,0:T(8,128)S(1)} %maximum_add_fusion.4, s32[]{:T(128)} %constant.135.clone.1..sunk, s32[]{:T(128)S(6)} %select_n.186, s32[]{:T(128)S(6)} %select_n.187) | dynamic-update-slice | bytes 1572868 | tf_op jit(solution)/shard_map/while/body/eval_jaxpr/dynamic_update_slice | solution.py:103
  157.8 2.9 fusion.247
  171.5 3.1 fusion.249
  177.3 3.3 add_bitcast_fusion.2
  182.2 3.3 maximum_add_fusion.5
  185.6 9.3 %dynamic_update_slice.10 = f32[3,640,640]{2,1,0:T(8,128)} dynamic-update-slice(f32[3,640,640]{2,1,0:T(8,128)} %get-tuple-element.586, f32[3,256,256]{2,1,0:T(8,128)S(1)} %maximum_add_fusion.4, s32[]{:T(128)} %constant.135.clone.1..sunk, s32[]{:T(128)S(6)} %select_n.186, s32[]{:T(128)S(6)} %select_n.187) | dynamic-update-slice | bytes 1572868 | tf_op jit(solution)/shard_map/while/body/eval_jaxpr/dynamic_update_slice | solution.py:103
  200.0 128.4 %all-reduce.4.cloned.1.call-done = f32[3,640,640]{2,1,0:T(8,128)} async-done(((f32[3,640,640]{2,1,0:T(8,128)}), f32[3,640,640]{2,1,0:T(8,128)}) %all-reduce.4.cloned.1.call-update) | async-done | bytes 4915216 | tf_op jit(solution)/shard_map/psum | solution.py:119
  330.2 3.5 collective-permute-start.2
  333.7 40.9 %collective-permute-done.2 = f32[3,640,256]{2,1,0:T(8,128)S(1)} collective-permute-done((f32[3,640,256]{2,1,0:T(8,128)S(1)}, f32[3,640,256]{2,1,0:T(8,128)S(1)}, u32[]{:S(2)}, u32[]{:S(2)}) %collective-permute-start.2) | collective-permute-done | bytes 1966112 | tf_op jit(solution)/shard_map/ppermute | solution.py:16
  375.9 4.1 collective-permute-start.3
  380.0 3.0 copy.25
  383.2 20.1 %collective-permute-done.3 = f32[3,256,384]{2,1,0:T(8,128)} collective-permute-done((f32[3,256,384]{2,1,0:T(8,128)}, f32[3,256,384]{2,1,0:T(8,128)}, u32[]{:S(2)}, u32[]{:S(2)}) %collective-permute-start.3) | collective-permute-done | bytes 1179680 | tf_op jit(solution)/shard_map/ppermute | solution.py:16
  405.0 4.2 collective-permute-start.4
  410.5 232.5 %all-reduce.6.cloned.1.call-done = (f32[4,2,256,256]{3,2,1,0:T(8,128)}, f32[256,256]{1,0:T(8,128)}) async-done(((f32[4,2,256,256]{3,2,1,0:T(8,128)}, f32[256,256]{1,0:T(8,128)}), (f32[4,2,256,256]{3,2,1,0:T(8,128)}, f32[256,256]{1,0:T(8,128)})) %all-reduce.6.cloned.1.call-update) | async-done | bytes 2359312 | tf_op jit(solution)/shard_map/psum | solution.py:118
  644.2 3.3 collective-permute-start.7
  647.5 3.2 divide_add_fusion
  654.5 6.5 collective-permute-done.6
  (97 shorter events, 107.7 us)
Async XLA Ops:
  8.0 2.6 copy-start.7
  8.0 320.4 %all-reduce.4.cloned.1.call-start = ((), (), s32[]{:S(2)}) async-start(), calls=%async_computation | async-start | bytes 9830400 | tf_op jit(solution)/shard_map/psum | solution.py:119
  9.3 19.0 %collective-permute-start = (f32[2,384,256]{2,1,0:T(8,128)S(1)}, f32[2,384,256]{2,1,0:T(8,128)S(1)}, u32[]{:S(2)}, u32[]{:S(2)}) collective-permute-start(f32[2,384,256]{2,1,0:T(8,128)S(1)} %slice.130), channel_id=1, source_target_pairs={{1,0},{2,1},{3,2},{5,4},{6,5},{7,6},{9,8},{10,9},{11,10},{13,12},{... | collective-permute-start | bytes 2359304 | tf_op jit(solution)/shard_map/ppermute | solution.py:16
  28.4 1.3 copy-start.4
  29.7 2.6 copy-start
  30.9 1.6 copy-start.9
  30.9 32.8 %collective-permute-start.1 = (f32[2,256,640]{2,1,0:T(8,128)}, f32[2,256,640]{2,1,0:T(8,128)}, u32[]{:S(2)}, u32[]{:S(2)}) collective-permute-start(f32[2,256,640]{2,1,0:T(8,128)} %slice.157), channel_id=1, source_target_pairs={{4,0},{8,4},{12,8},{5,1},{9,5},{13,9},{6,2},{10,6},{14,10},{7,3},{... | collective-permute-start | bytes 3932168 | tf_op jit(solution)/shard_map/ppermute | solution.py:16
  32.3 1.6 copy-start.1
  33.9 29.8 %copy-start.5 = (f32[2,384,640]{2,1,0:T(8,128)S(1)}, f32[2,384,640]{2,1,0:T(8,128)}, u32[]{:S(2)}) copy-start(f32[2,384,640]{2,1,0:T(8,128)} %copy-done.4) | copy-start | bytes 5898244
  66.9 2.5 copy-start.10
  199.3 0.7 copy-start.6
  200.0 443.0 %all-reduce.6.cloned.1.call-start = ((), (), s32[]{:S(2)}) async-start(), calls=%async_computation.1 | async-start | bytes 4718592 | tf_op jit(solution)/shard_map/psum | solution.py:118
  328.4 46.2 %copy-start.3 = (f32[3,640,640]{2,1,0:T(8,128)S(1)}, f32[3,640,640]{2,1,0:T(8,128)}, u32[]{:S(2)}) copy-start(f32[3,640,640]{2,1,0:T(8,128)} %all-reduce.4.cloned.1.call-done) | copy-start | bytes 14745604
  330.2 44.4 %slice-start = ((f32[3,640,640]{2,1,0:T(8,128)}), f32[3,640,384]{2,1,0:T(8,128)S(1)}, s32[]{:S(2)}) async-start(f32[3,640,640]{2,1,0:T(8,128)} %all-reduce.4.cloned.1.call-done), calls=%async_computation.2 | async-start | bytes 5898240 | tf_op jit(solution)/shard_map/slice | solution.py:50
  330.2 44.4 %collective-permute-start.2 = (f32[3,640,256]{2,1,0:T(8,128)S(1)}, f32[3,640,256]{2,1,0:T(8,128)S(1)}, u32[]{:S(2)}, u32[]{:S(2)}) collective-permute-start(f32[3,640,256]{2,1,0:T(8,128)S(1)} %slice.160), channel_id=1, source_target_pairs={{0,1},{1,2},{2,3},{4,5},{5,6},{6,7},{8,9},{9,10},{10,11},{12,13},{... | collective-permute-start | bytes 5898248 | tf_op jit(solution)/shard_map/ppermute | solution.py:16
  375.9 27.4 %collective-permute-start.3 = (f32[3,256,384]{2,1,0:T(8,128)}, f32[3,256,384]{2,1,0:T(8,128)}, u32[]{:S(2)}, u32[]{:S(2)}) collective-permute-start(f32[3,256,384]{2,1,0:T(8,128)} %slice.163), channel_id=1, source_target_pairs={{0,4},{4,8},{8,12},{1,5},{5,9},{9,13},{2,6},{6,10},{10,14},{3,7},{... | collective-permute-start | bytes 3538952 | tf_op jit(solution)/shard_map/ppermute | solution.py:16
  383.2 21.6 %copy-start.8 = (f32[2,384,384]{2,1,0:T(8,128)S(1)}, f32[2,384,384]{2,1,0:T(8,128)}, u32[]{:S(2)}) copy-start(f32[2,384,384]{2,1,0:T(8,128)} %param.11) | copy-start | bytes 3538948
  405.0 242.5 %copy-start.2 = (f32[4,2,256,256]{3,2,1,0:T(8,128)S(1)}, f32[4,2,256,256]{3,2,1,0:T(8,128)}, u32[]{:S(2)}) copy-start(f32[4,2,256,256]{3,2,1,0:T(8,128)} %param.12) | copy-start | bytes 6291460
  405.0 239.0 %collective-permute-start.4 = (f32[2,1,384]{2,1,0:T(1,128)S(1)}, f32[2,1,384]{2,1,0:T(1,128)S(1)}, u32[]{:S(2)}, u32[]{:S(2)}) collective-permute-start(f32[2,1,384]{2,1,0:T(1,128)S(1)} %get-tuple-element.461), channel_id=1, source_target_pairs={{0,4},{4,8},{8,12},{1,5},{5,9},{9,13},{2,6},{6,10},{10,14},{3,7},{... | collective-permute-start | bytes 9224 | tf_op jit(solution)/shard_map/ppermute | solution.py:26
  409.2 234.7 %collective-permute-start.5 = (f32[2,1,384]{2,1,0:T(1,128)S(1)}, f32[2,1,384]{2,1,0:T(1,128)S(1)}, u32[]{:S(2)}, u32[]{:S(2)}) collective-permute-start(f32[2,1,384]{2,1,0:T(1,128)S(1)} %get-tuple-element.462), channel_id=1, source_target_pairs={{4,0},{8,4},{12,8},{5,1},{9,5},{13,9},{6,2},{10,6},{14,10},{7,3},{... | collective-permute-start | bytes 9224 | tf_op jit(solution)/shard_map/ppermute | solution.py:27
  644.2 9.8 %collective-permute-start.7 = (f32[2,386,1]{2,1,0:T(8,128)S(1)}, f32[2,386,1]{2,1,0:T(8,128)S(1)}, u32[]{:S(2)}, u32[]{:S(2)}) collective-permute-start(f32[2,386,1]{2,1,0:T(8,128)S(1)} %get-tuple-element.460), channel_id=1, source_target_pairs={{0,1},{1,2},{2,3},{4,5},{5,6},{6,7},{8,9},{9,10},{10,11},{12,13},{... | collective-permute-start | bytes 9272 | tf_op jit(solution)/shard_map/ppermute | solution.py:26
  650.7 10.3 %collective-permute-start.6 = (f32[2,386,1]{2,1,0:T(8,128)S(1)}, f32[2,386,1]{2,1,0:T(8,128)S(1)}, u32[]{:S(2)}, u32[]{:S(2)}) collective-permute-start(f32[2,386,1]{2,1,0:T(8,128)S(1)} %get-tuple-element.459), channel_id=1, source_target_pairs={{1,0},{2,1},{3,2},{5,4},{6,5},{7,6},{9,8},{10,9},{11,10},{13,12},{... | collective-permute-start | bytes 9272 | tf_op jit(solution)/shard_map/ppermute | solution.py:27
Sparse Core Ops, SparseCore 0:
  199.4 128.9 all-reduce.3
Sparse Core Ops, SparseCore 1:
  383.2 259.7 all-reduce.5
where the time goes:
time: 677 us; the launch traced here: 672 us
  waiting for transfers between devices  478 us (71%)
  matrix products  88.8 us (13%)
  local copies, waits for them, and re-layouts  34.3 us (5%)
  other arithmetic  27.2 us (4%)
  starting transfers between devices  20.5 us (3%)
  between operations  16 us (2%)
  loops' own time  7.74 us (1%)
    psum x1, waiting for transfers between devices, body(): numer, denom = lax.psum((numer, denom), ('pos', 'ty', 'tx'))  232 us
    psum x1, waiting for transfers between devices, body(): accum = lax.psum(accum, 'pos')  128 us
    ppermute x4, waiting for transfers between devices, passed_along(): return lax.ppermute(x, axis, pairs)  108 us
    dot_general x16, matrix products, right_product(): jnp.einsum('mkn,nl->mkl', field, table, precision=lax.Precision.HIGHEST)  44.9 us
    dot_general x16, matrix products, left_product(): jnp.einsum('kn,mnl->mkl', table, field, precision=lax.Precision.HIGHEST)  43.9 us
    dynamic_update_slice x2, local copies, waits for them, and re-layouts, visit(): lax.dynamic_update_slice(accum, region + terms, (zero_index, local_row, l...  18.3 us
  transfers between devices with their start and end apart: 10, of which 8 were waited for; matrix products, arithmetic and copies ran while one was open for 1% of the time, Pallas kernels for 0%

commit v1 on v0

v1 whole, which is shorter than its diff:
```python
import functools, math
import numpy as np, ml_dtypes
import jax, jax.numpy as jnp
from jax import lax
from jax.experimental import pallas as pl
from jax.experimental.pallas import tpu as pltpu
from jax.sharding import PartitionSpec as P

N = 256
H = 128
TILE = 384
EXT = 640
intensity_floor = 0.25
flux_floor = 0.25
tv_weight = 0.1
N_POS, N_Y, N_X = 16, 4, 4
f32, bf16 = jnp.float32, jnp.bfloat16


def tables():
    k = np.arange(H)
    ang = 2.0 * np.pi * ((k[:, None] * k[None, :]) % H) / H
    c, s = np.cos(ang) / 16.0, np.sin(ang) / 16.0
    m = np.block([[c, -s], [s, c]]).astype(np.float32)
    hi = m.astype(ml_dtypes.bfloat16)
    lo = (m - hi.astype(np.float32)).astype(ml_dtypes.bfloat16)
    fwd_right = np.concatenate([hi, hi, lo], 0)
    inv_right = np.concatenate([hi.T, hi.T, lo.T], 0)
    fwd_left = np.concatenate([hi.T, hi.T, lo.T], 1)
    inv_left = np.concatenate([hi, hi, lo], 1)
    th = 2.0 * np.pi * k / N
    tw = np.stack([np.cos(th), np.sin(th)]).astype(np.float32)
    lane_tw = np.stack([np.tile(tw[0], (8, 1)), np.tile(tw[1], (8, 1))])
    row_tw = np.stack([np.tile(tw[0][:, None], (1, H)), np.tile(tw[1][:, None], (1, H))])
    perm = np.concatenate([np.arange(0, N, 2), np.arange(1, N, 2)])
    pick = np.zeros((N, N), np.float32)
    pick[np.arange(N), perm] = 1.0
    pick = pick.astype(ml_dtypes.bfloat16)
    return fwd_right, inv_right, fwd_left, inv_left, lane_tw, row_tw, pick, pick.T.copy()


def split(x):
    hi = x.astype(bf16)
    lo = (x - hi.astype(f32)).astype(bf16)
    return hi, lo


def right(x, table):
    hi, lo = split(x)
    return jnp.dot(jnp.concatenate([hi, lo, hi], 1), table, preferred_element_type=f32)


def left(table, x):
    hi, lo = split(x)
    return jnp.dot(table, jnp.concatenate([hi, lo, hi], 0), preferred_element_type=f32)


def split_dot_l(p, x):
    hi, lo = split(x)
    return jnp.dot(p, hi, preferred_element_type=f32) + jnp.dot(p, lo, preferred_element_type=f32)


def split_dot_r(x, p):
    hi, lo = split(x)
    return jnp.dot(hi, p, preferred_element_type=f32) + jnp.dot(lo, p, preferred_element_type=f32)


def shift_up_left(x, srow, scol):
    lane = lax.broadcasted_iota(jnp.int32, (N + 8, 128), 1)
    back = lax.rem(128 - scol, 128)
    turned = [pltpu.roll(x[:, 128 * i:128 * (i + 1)], back, 1) for i in range(3)]
    keep = lane < 128 - scol
    x = jnp.concatenate([jnp.where(keep, turned[i], turned[i + 1]) for i in range(2)], 1)
    x = x.reshape(N // 8 + 1, 8, N)
    x = pltpu.roll(x, lax.rem(8 - srow, 8), 1)
    sub = lax.broadcasted_iota(jnp.int32, (N // 8, 8, N), 1)
    return jnp.where(sub < 8 - srow, x[:-1], x[1:]).reshape(N, N)


def shift_down_right(x, srow, scol):
    x = pltpu.roll(x.reshape(N // 8, 8, N), srow, 1)
    none = jnp.zeros((1, 8, N), f32)
    sub = lax.broadcasted_iota(jnp.int32, (N // 8 + 1, 8, N), 1)
    x = jnp.where(sub >= srow, jnp.concatenate([x, none], 0), jnp.concatenate([none, x], 0))
    x = x.reshape(N + 8, N)
    lane = lax.broadcasted_iota(jnp.int32, (N + 8, 128), 1)
    t = [pltpu.roll(x[:, 128 * i:128 * (i + 1)], scol, 1) for i in range(2)]
    keep = lane >= scol
    return jnp.concatenate([jnp.where(keep, t[0], 0.0), jnp.where(keep, t[1], t[0]), jnp.where(keep, 0.0, t[1])], 1)


def compute_kernel(slots, offs, ext, probe, amps, live, fr, ir, fl, il, ltw, rtw, pick, pick_t,
                   frame, sums,
                   patch, far, fac, grad, weight, mask):
    modes = probe.shape[0]
    frame[...] = jnp.zeros_like(frame)
    sums[...] = jnp.zeros_like(sums)
    w = jnp.zeros((N, N), f32)
    for m in range(modes):
        w = w + (probe[m, 0] * probe[m, 0] + probe[m, 1] * probe[m, 1])
    weight[...] = w
    on = (live[...] == 1).astype(bf16)
    on = jnp.dot(pick[...], on, preferred_element_type=f32).astype(bf16)
    mask[...] = jnp.dot(on, pick_t[...], preferred_element_type=f32)

    @pl.loop(0, slots)
    def _(p):
        row, col = offs[p, 0], offs[p, 1]
        row8, col128 = row // 8, col // 128
        srow, scol = row - row8 * 8, col - col128 * 128
        rows = pl.ds(pl.multiple_of(row8 * 8, 8), N + 8)
        cols = pl.ds(pl.multiple_of(col128 * 128, 128), N + 128)
        for c in range(2):
            patch[c] = shift_up_left(ext[c, rows, cols], srow, scol)
        pr, pi = patch[0], patch[1]
        sums[2 * modes] += pr * pr + pi * pi
        grad[...] = jnp.zeros_like(grad)
        fac[...] = jnp.zeros_like(fac)

        @pl.loop(0, modes, unroll=4)
        def _(m):
            pr, pi = patch[0], patch[1]
            qr, qi = probe[m, 0], probe[m, 1]
            wr = qr * pr - qi * pi
            wi = qr * pi + qi * pr
            ar, ai = wr[:, :H] + wr[:, H:], wi[:, :H] + wi[:, H:]
            br, bi = wr[:, :H] - wr[:, H:], wi[:, :H] - wi[:, H:]
            tc, ts = ltw[0, 0:1], ltw[1, 0:1]
            br, bi = br * tc + bi * ts, bi * tc - br * ts
            even = right(jnp.concatenate([ar, ai], 1), fr[...])
            odd = right(jnp.concatenate([br, bi], 1), fr[...])
            total = None
            rc, rs = rtw[0], rtw[1]
            for h, z in enumerate((even, odd)):
                zr, zi = z[:, :H], z[:, H:]
                ar, ai = zr[:H] + zr[H:], zi[:H] + zi[H:]
                br, bi = zr[:H] - zr[H:], zi[:H] - zi[H:]
                br, bi = br * rc + bi * rs, bi * rc - br * rs
                both = jnp.concatenate([jnp.concatenate([ar, br], 1), jnp.concatenate([ai, bi], 1)], 0)
                out = left(fl[...], both)
                far[m, h] = out
                sq = out * out
                power = sq[:H] + sq[H:]
                fac[h] += power

        amp = split_dot_r(split_dot_l(pick[...], amps[p]), pick_t[...])
        for h in range(2):
            want = jnp.concatenate([amp[:H, h * H:(h + 1) * H], amp[H:, h * H:(h + 1) * H]], 1)
            lv = jnp.concatenate([mask[:H, h * H:(h + 1) * H], mask[H:, h * H:(h + 1) * H]], 1)
            fac[h] = jnp.where(lv > 0.5, want * lax.rsqrt(jnp.maximum(fac[h], intensity_floor)), 1.0)

        @pl.loop(0, modes, unroll=4)
        def _(m):
            rc, rs = rtw[0], rtw[1]
            halves = []
            for h in range(2):
                f = far[m, h]
                k = fac[h]
                y = jnp.concatenate([f[:H] * k, f[H:] * k], 0)
                x = left(il[...], y)
                er, orr = x[:H, :H], x[:H, H:]
                ei, oi = x[H:, :H], x[H:, H:]
                orr, oi = orr * rc - oi * rs, oi * rc + orr * rs
                top = jnp.concatenate([er + orr, ei + oi], 1)
                bottom = jnp.concatenate([er - orr, ei - oi], 1)
                halves.append(right(jnp.concatenate([top, bottom], 0), ir[...]))
            e, o = halves
            er, ei, orr, oi = e[:, :H], e[:, H:], o[:, :H], o[:, H:]
            tc, ts = ltw[0, 0:1], ltw[1, 0:1]
            orr, oi = orr * tc - oi * ts, oi * tc + orr * ts
            nr = jnp.concatenate([er + orr, er - orr], 1)
            ni = jnp.concatenate([ei + oi, ei - oi], 1)
            pr, pi = patch[0], patch[1]
            qr, qi = probe[m, 0], probe[m, 1]
            dr = nr - (qr * pr - qi * pi)
            di = ni - (qr * pi + qi * pr)
            grad[0] += qr * dr + qi * di
            grad[1] += qr * di - qi * dr
            sums[2 * m] += pr * dr + pi * di
            sums[2 * m + 1] += pr * di - pi * dr

        for c in range(frame.shape[0]):
            frame[c, rows, cols] += shift_down_right(grad[c] if c < 2 else weight[...], srow, scol)


def compute_call(offs, ext, probe, amps, live, channels=3):
    slots = amps.shape[0]
    modes = probe.shape[0]
    vm = pl.BlockSpec(memory_space=pltpu.VMEM)
    consts = [jnp.asarray(t) for t in tables()]
    return pl.pallas_call(
        functools.partial(compute_kernel, slots),
        out_shape=(
            jax.ShapeDtypeStruct((channels, EXT, EXT), f32),
            jax.ShapeDtypeStruct((2 * modes + 1, N, N), f32),
        ),
        in_specs=[pl.BlockSpec(memory_space=pltpu.SMEM)] + [vm] * (4 + len(consts)),
        out_specs=(vm, vm),
        scratch_shapes=[
            pltpu.VMEM((2, N, N), f32),
            pltpu.VMEM((modes, 2, N, N), f32),
            pltpu.VMEM((2, H, N), f32),
            pltpu.VMEM((2, N, N), f32),
            pltpu.VMEM((N, N), f32),
            pltpu.VMEM((N, N), f32),
        ],
        compiler_params=pltpu.CompilerParams(vmem_limit_bytes=50 * 2**20),
        name="positions",
    )(offs, ext, probe, amps, live, *consts)


MESH = pl.DeviceIdType.MESH


class Wires:
    def __init__(self, send, recv):
        self.send, self.recv, self.count, self.started = send, recv, 0, []

    def slot(self):
        self.count += 1
        return self.count - 1

    def copy(self, src, dst, slot, to):
        return pltpu.make_async_remote_copy(
            src_ref=src, dst_ref=dst, send_sem=self.send.at[slot], recv_sem=self.recv.at[slot],
            device_id=to, device_id_type=MESH)

    def start(self, src, dst, slot, to):
        made = self.copy(src, dst, slot, to)
        made.start()
        self.started.append(made)
        return made

    def finish(self):
        for made in self.started:
            made.wait_send()


def greet(partners):
    barrier = pltpu.get_barrier_semaphore()
    for to in partners:
        pl.semaphore_signal(barrier, inc=1, device_id=to, device_id_type=MESH)
    pl.semaphore_wait(barrier, len(partners))


def places():
    p = lax.axis_index("pos")
    return p, p // 2, lax.rem(p, 2), lax.axis_index("ty"), lax.axis_index("tx")


def halo_kernel(obj, ext, here, send, recv):
    p, z, c, a, b = places()
    tile = obj.shape[1]
    up, down = lax.rem(a + N_Y - 1, N_Y), lax.rem(a + 1, N_Y)
    left, right_ = lax.rem(b + N_X - 1, N_X), lax.rem(b + 1, N_X)
    sib = {"pos": 2 * z + 1 - c}
    greet([sib, {"tx": left}, {"tx": right_}, {"ty": up}, {"ty": down},
           {"ty": up, "tx": left}, {"ty": down, "tx": right_}])
    w = Wires(send, recv)
    own = pltpu.make_async_copy(obj, ext.at[:, 0:tile, 0:tile], here)
    own.start()
    parts = [
        (obj.at[c, 0:N, 0:N], (pl.ds(tile, N), pl.ds(tile, N)), {"ty": up, "tx": left}),
        (obj.at[c, :, 0:N], (pl.ds(0, tile), pl.ds(tile, N)), {"tx": left}),
        (obj.at[c, 0:N, :], (pl.ds(tile, N), pl.ds(0, tile)), {"ty": up}),
    ]
    got = []
    for src, (rows, cols), to in parts:
        got.append(w.start(src, ext.at[c, rows, cols], w.slot(), to))
    shared = []
    for made, (src, (rows, cols), to) in list(zip(got, parts)):
        made.wait_recv()
        shared.append(w.start(ext.at[c, rows, cols], ext.at[c, rows, cols], w.slot(), sib))
    for made in shared:
        made.wait_recv()
    own.wait()
    w.finish()


def halo_call(obj):
    return pl.pallas_call(
        halo_kernel,
        out_shape=jax.ShapeDtypeStruct((2, EXT, EXT), f32),
        in_specs=[pl.BlockSpec(memory_space=pltpu.VMEM)],
        out_specs=pl.BlockSpec(memory_space=pltpu.VMEM),
        scratch_shapes=[pltpu.SemaphoreType.DMA, pltpu.SemaphoreType.DMA((6,)), pltpu.SemaphoreType.DMA((6,))],
        compiler_params=pltpu.CompilerParams(collective_id=0, has_side_effects=True, vmem_limit_bytes=32 * 2**20),
        name="halo",
    )(obj)


def merge_kernel(channels, frame, sums, obj, probe, out, pout,
                 s, rin, lin, t, fr, fb, fc, acc, wide, hl, hr, tops, bots, up_in, up_edge, dn_in, dn_edge,
                 r0, pa, q, pb, tt, st, pz, send, recv):
    p, z, c, a, b = places()
    nz = N_POS // 2
    half = nz // 2
    up, down = lax.rem(a + N_Y - 1, N_Y), lax.rem(a + 1, N_Y)
    left, right_ = lax.rem(b + N_X - 1, N_X), lax.rem(b + 1, N_X)
    following, previous = lax.rem(p + 1, N_POS), lax.rem(p + N_POS - 1, N_POS)

    def zat(k):
        return lax.rem(z + (k + nz), nz)

    def zdev(k):
        return {"pos": 2 * zat(k) + c}

    sib = {"pos": 2 * z + 1 - c}
    greet([sib] + [zdev(k) for k in range(1, nz)]
          + [{"ty": lax.rem(a + k, N_Y)} for k in range(1, N_Y)]
          + [{"tx": lax.rem(b + k, N_X)} for k in range(1, N_X)]
          + [{"ty": down, "tx": right_}, {"ty": up, "tx": left}]
          + [{"pos": following}, {"pos": previous}]
          + [{"pos": N_POS - 1 - p, "ty": down}, {"pos": N_POS - 1 - p, "ty": up}])
    w = Wires(send, recv)
    up_edge[...] = jnp.zeros_like(up_edge)
    dn_edge[...] = jnp.zeros_like(dn_edge)
    total = frame.shape[0]
    cut = (total + 1) // 2
    parts = (pl.ds(0, cut), pl.ds(cut, total - cut))

    def object_path():
        order = [half]
        for k in range(half - 1, 0, -1):
            order += [k, -k]
        order += [0]
        swaps = {k: w.start(frame.at[:, zat(k), 1 - c], s.at[zat(k)], w.slot(), sib) for k in order}
        yield

        def mine(k):
            swaps[k].wait_recv()
            s[zat(k)] += frame[:, zat(k), c]

        went = {}
        for step in range(half):
            for k in ((half,) if step == 0 else (half - step, step - half)):
                mine(k)
            for part in range(2):
                for way, box in ((1, rin), (-1, lin)):
                    if step == 0 and part != (0 if way == 1 else 1):
                        continue
                    d = zat(way * (half - step))
                    before = went.get((step - 1, way, part))
                    if before is not None:
                        before.wait_recv()
                        s[d, parts[part]] += box[step - 1, parts[part]]
                    went[step, way, part] = w.start(
                        s.at[d, parts[part]], box.at[step, parts[part]], w.slot(), zdev(way))
            yield
        mine(0)
        last = half - 1
        for part in range(2):
            for way, box in ((1, rin), (-1, lin)):
                went[last, way, part].wait_recv()
                s[z, parts[part]] += box[last, parts[part]]
        t[...] = s[z].reshape(channels, 5, 8, EXT)
        f1 = w.start(t.at[:, 0:3, :, TILE:EXT], fr, w.slot(), {"tx": right_})
        f2 = w.start(t.at[:, 3:5, :, 0:TILE], fb, w.slot(), {"ty": down})
        f3 = w.start(t.at[:, 3:5, :, TILE:EXT], fc, w.slot(), {"ty": down, "tx": right_})
        yield
        acc[...] = t[:, 0:3, :, 0:TILE]
        f1.wait_recv()
        acc[:, :, :, 0:N] += fr[...]
        f2.wait_recv()
        acc[:, 0:2] += fb[...]
        f3.wait_recv()
        acc[:, 0:2, :, 0:N] += fc[...]
        share = acc[2] + 1.0
        for ch in range(2):
            wide[ch, :, :, 128:128 + TILE] = obj[ch, :, p] + acc[ch] / share
        h1 = w.start(wide.at[:, :, :, TILE:TILE + 128], hl, w.slot(), {"tx": right_})
        h2 = w.start(wide.at[:, :, :, 128:256], hr, w.slot(), {"tx": left})
        yield
        h1.wait_recv()
        wide[:, :, :, 0:128] = jnp.where(b > 0, hl[...], 0.0)
        h2.wait_recv()
        wide[:, :, :, 128 + TILE:] = jnp.where(b < N_X - 1, hr[...], 0.0)
        tops[...] = jnp.zeros_like(tops)
        bots[...] = jnp.zeros_like(bots)
        for ch in range(2):
            for g in range(3):
                k = 3 * ch + g
                tops[k:k + 1, :] = wide[ch, g, 0:1, :]
                bots[k:k + 1, :] = wide[ch, g, 7:8, :]
        v1 = w.start(bots, up_in, w.slot(), {"pos": following})
        v2 = w.start(tops, dn_in, w.slot(), {"pos": previous})
        k3, k4 = w.slot(), w.slot()

        @pl.when(p == N_POS - 1)
        def _():
            w.copy(bots, up_edge, k3, {"pos": 0, "ty": down}).start()

        @pl.when(p == 0)
        def _():
            w.copy(tops, dn_edge, k4, {"pos": N_POS - 1, "ty": up}).start()

        yield
        v1.wait_recv()
        v2.wait_recv()

        @pl.when(p == 0)
        def _():
            made = w.copy(bots, up_edge, k3, {"pos": 0, "ty": down})
            made.wait_recv()
            w.copy(tops, dn_edge, k4, {"pos": N_POS - 1, "ty": up}).wait_send()

        @pl.when(p == N_POS - 1)
        def _():
            w.copy(tops, dn_edge, k4, {"pos": N_POS - 1, "ty": up}).wait_recv()
            w.copy(bots, up_edge, k3, {"pos": 0, "ty": down}).wait_send()

        sub = lax.broadcasted_iota(jnp.int32, (8, EXT), 0)

        def unit(x, below):
            fx = [pltpu.roll(v, EXT - 1, 1) - v for v in x]
            fy = [n - v for v, n in zip(x, below)]
            power = fx[0] * fx[0] + fy[0] * fy[0] + fx[1] * fx[1] + fy[1] * fy[1]
            mag = jnp.sqrt(jnp.maximum(power, flux_floor))
            return [v / mag for v in fx], [v / mag for v in fy]

        for g in range(3):
            x, above, below = [], [], []
            for ch in range(2):
                k = 3 * ch + g
                v = wide[ch, g]
                if g == 0:
                    edge = jnp.where(a > 0, up_edge[3 * ch + 2:3 * ch + 3, :], 0.0)
                else:
                    edge = up_in[k - 1:k, :]
                first = jnp.where(p == 0, edge, up_in[k:k + 1, :])
                if g == 2:
                    edge = jnp.where(a < N_Y - 1, dn_edge[3 * ch:3 * ch + 1, :], 0.0)
                else:
                    edge = dn_in[k + 1:k + 2, :]
                final = jnp.where(p == N_POS - 1, edge, dn_in[k:k + 1, :])
                x.append(v)
                above.append(jnp.where(sub == 0, first, pltpu.roll(v, 1, 0)))
                below.append(jnp.where(sub == 7, final, pltpu.roll(v, 7, 0)))
            nx, ny = unit(x, below)
            _, my = unit(above, x)
            for ch in range(2):
                div = nx[ch] - pltpu.roll(nx[ch], 1, 1) + ny[ch] - my[ch]
                out[ch, g, p] = (x[ch] + tv_weight * div)[:, 128:128 + TILE]
        went, twin = {}, []

        def twin_send(k):
            q_ = 2 * zat(k) + c
            twin.append(w.start(out.at[:, :, q_], out.at[:, :, q_], w.slot(), sib))

        for step in range(half):
            for way in (1, -1):
                q_ = 2 * zat(-way * step) + c
                for ch in range(2):
                    if step == half - 1 and ch != (0 if way == 1 else 1):
                        continue
                    if step > 0:
                        went[step - 1, way, ch].wait_recv()
                    went[step, way, ch] = w.start(out.at[ch, :, q_], out.at[ch, :, q_], w.slot(), zdev(way))
                if step == half - 1:
                    went[step - 1, way, 1 if way == 1 else 0].wait_recv()
                if step == 0:
                    if way == 1:
                        twin_send(0)
                else:
                    twin_send(-way * step)
            yield
        went[half - 1, 1, 0].wait_recv()
        went[half - 1, -1, 1].wait_recv()
        twin_send(half)
        yield
        for made in twin:
            made.wait_recv()
        yield

    lanes = pl.ds(pl.multiple_of(c * 128, 128), 128)
    others = pl.ds(pl.multiple_of((1 - c) * 128, 128), 128)

    def at_y(k):
        return lax.rem(a + (k + N_Y), N_Y)

    def at_x(k):
        return lax.rem(b + (k + N_X), N_X)

    def probe_path():
        swap = w.start(sums.at[:, :, :, :, :, others], r0, w.slot(), sib)
        yield
        swap.wait_recv()
        r0[...] += sums[:, :, :, :, :, lanes]
        first = []
        for k in range(1, N_Y):
            first.append((0, k, w.start(r0.at[:, at_y(k), :, 0], pa.at[0, k - 1], w.slot(), {"ty": at_y(k)})))
        for k in range(1, N_X):
            first.append((1, k, w.start(r0.at[:, :, at_x(k), 1], pa.at[1, k - 1], w.slot(), {"tx": at_x(k)})))
        yield
        q[0] = r0[:, a, :, 0]
        q[1] = r0[:, :, b, 1]
        for i, k, made in first:
            made.wait_recv()
            q[i] += pa[i, k - 1]
        second = []
        for k in range(1, N_X):
            second.append((0, k, w.start(q.at[0, :, at_x(k)], pb.at[0, k - 1], w.slot(), {"tx": at_x(k)})))
        for k in range(1, N_Y):
            second.append((1, k, w.start(q.at[1, :, at_y(k)], pb.at[1, k - 1], w.slot(), {"ty": at_y(k)})))
        yield
        tt[:, 0] = q[0, :, b]
        tt[:, 1] = q[1, :, a]
        for i, k, made in second:
            made.wait_recv()
            tt[:, i] += pb[i, k - 1]
        st[:, 0] = tt[0:8]
        for k in range(nz):
            st[k, 1] = tt[8]
        third = [w.start(st.at[zat(k)], pz.at[k - 1], w.slot(), zdev(k)) for k in range(1, nz)]
        yield
        whole = st[z]
        for k in range(1, nz):
            third[k - 1].wait_recv()
            whole = whole + pz[k - 1]
        pout[z, a, b, :, :, lanes] = probe[z, a, b, :, :, lanes] + whole[0] / (whole[1] + 1.0)
        spot = pout.at[z, a, b, :, :, lanes]
        fourth = [w.start(spot, spot, w.slot(), zdev(k)) for k in range(1, nz)]
        yield
        for made in fourth:
            made.wait_recv()
        fifth = []
        spot = pout.at[:, a, b, 0, :, lanes]
        for k in range(1, N_X):
            fifth.append(w.start(spot, spot, w.slot(), {"tx": at_x(k)}))
        spot = pout.at[:, a, b, 1, :, lanes]
        for k in range(1, N_Y):
            fifth.append(w.start(spot, spot, w.slot(), {"ty": at_y(k)}))
        yield
        for made in fifth:
            made.wait_recv()
        sixth = []
        spot = pout.at[:, a, :, 0, :, lanes]
        for k in range(1, N_Y):
            sixth.append(w.start(spot, spot, w.slot(), {"ty": at_y(k)}))
        spot = pout.at[:, :, b, 1, :, lanes]
        for k in range(1, N_X):
            sixth.append(w.start(spot, spot, w.slot(), {"tx": at_x(k)}))
        yield
        for made in sixth:
            made.wait_recv()
        spot = pout.at[:, :, :, :, :, lanes]
        last = w.start(spot, spot, w.slot(), sib)
        yield
        last.wait_recv()
        yield

    objects, probes = object_path(), probe_path()
    for turn in MERGE_ORDER:
        next({"o": objects, "p": probes}[turn])
    for path in (objects, probes):
        for _ in path:
            pass
    w.finish()


MERGE_ORDER = "opo" + "po" + "opo" + "pop" + "opopo" + "oo"
MERGE_WIRES = 110


def merge_call(frame, sums, obj, probe):
    channels = frame.shape[0]
    vm = pl.BlockSpec(memory_space=pltpu.VMEM)
    nz = N_POS // 2
    g = 5 * channels
    half = nz // 2

    def v(*shape):
        return pltpu.VMEM(shape, f32)

    out, pout = pl.pallas_call(
        functools.partial(merge_kernel, channels),
        out_shape=(
            jax.ShapeDtypeStruct((2, 3, N_POS, 8, TILE), f32),
            jax.ShapeDtypeStruct((8, N_Y, N_X, 2, 8, N), f32),
        ),
        in_specs=[vm] * 4,
        out_specs=(vm, vm),
        scratch_shapes=[
            v(nz, g, 8, EXT), v(half, g, 8, EXT), v(half, g, 8, EXT), v(channels, 5, 8, EXT),
            v(channels, 3, 8, N), v(channels, 2, 8, TILE), v(channels, 2, 8, N), v(channels, 3, 8, TILE),
            v(2, 3, 8, EXT), v(2, 3, 8, 128), v(2, 3, 8, 128),
            v(8, EXT), v(8, EXT), v(8, EXT), v(8, EXT), v(8, EXT), v(8, EXT),
            v(9, N_Y, N_X, 2, 8, 128), v(2, 3, 9, 4, 8, 128), v(2, 9, 4, 8, 128), v(2, 3, 9, 8, 128),
            v(9, 2, 8, 128), v(8, 2, 2, 8, 128), v(7, 2, 2, 8, 128),
            pltpu.SemaphoreType.DMA((MERGE_WIRES,)), pltpu.SemaphoreType.DMA((MERGE_WIRES,)),
        ],
        compiler_params=pltpu.CompilerParams(collective_id=1, has_side_effects=True, vmem_limit_bytes=56 * 2**20),
        name="merge",
    )(frame.reshape(g, nz, 2, 8, EXT), sums.reshape(9, N_Y, N_X, 2, 8, N),
      obj.reshape(2, 3, N_POS, 8, TILE), probe.reshape(8, N_Y, N_X, 2, 8, N))
    return out.reshape(2, TILE, TILE), pout.reshape(probe.shape)


def body(object_field, probe, amplitudes, live_pixels, offsets):
    base = jnp.stack([lax.axis_index("ty"), lax.axis_index("tx")]).astype(jnp.int32) * TILE
    ext = halo_call(object_field)
    frame, sums = compute_call(offsets - base, ext, probe, amplitudes, live_pixels)
    return merge_call(frame, sums, object_field, probe)


def solution(mesh):
    return jax.shard_map(
        body,
        mesh=mesh,
        in_specs=(
            P(None, "ty", "tx"),
            P(),
            P(("pos", "ty", "tx"), None, None),
            P(),
            P(("pos", "ty", "tx"), None),
        ),
        out_specs=(P(None, "ty", "tx"), P()),
        check_vma=False,
    )
```

time: 677 us -> 128 us (0.19)
  waiting for transfers between devices: 478 us -> 0 us
  Pallas kernels: 0 us -> 119 us
  matrix products: 88.8 us -> 0 us
  local copies, waits for them, and re-layouts: 34.3 us -> 6.85 us
  other arithmetic: 27.2 us -> 0.76 us
  starting transfers between devices: 20.5 us -> 0 us
  between operations: 16 us -> 0.77 us
  loops' own time: 7.74 us -> 0 us
    psum x2 -> x0, waiting for transfers between devices: 361 us -> none  [the longest x1 232 us: body(): numer, denom = lax.psum((numer, denom), ('pos', 'ty', 'tx'))]
    pallas_call x0 -> x3, Pallas kernels: none -> 119 us  [the longest x1 77.1 us: merge_call(): pl.pallas_call(functools.partial(merge_kernel, channels), out_shape=(jax....]
    ppermute x8 -> x0, waiting for transfers between devices: 117 us -> none  [the longest x4 108 us: passed_along(): return lax.ppermute(x, axis, pairs)]
    dot_general x32 -> x0, matrix products: 88.8 us -> none  [the longest x16 44.9 us: right_product(): jnp.einsum('mkn,nl->mkl', field, table, precision=lax.Precision.HIGHEST)]
    ppermute x8 -> x0, starting transfers between devices: 20.4 us -> none  [the longest x4 10.3 us: passed_along(): return lax.ppermute(x, axis, pairs)]
    dynamic_update_slice x2 -> x0, local copies, waits for them, and re-layouts: 18.3 us -> none  [visit(): lax.dynamic_update_slice(accum, region + terms, (zero_index, local_row, l...]
    add x10 -> x0, other arithmetic: 17.5 us -> none  [the longest x2 5.08 us: visit(): numer + jnp.stack([patch_real * delta_real + patch_imag * delta_imag, pat...]
    another operation x1 -> x0, loops' own time: 7.74 us -> none  [body(): lax.fori_loop(0, slots, visit, (accum0, numer0, denom0))]
  transfers between devices with their start and end apart: 10 -> 0, of which waited for: 8 -> 0; matrix products, arithmetic and copies ran while one was open for 1% -> 0% of each run, Pallas kernels for 0% -> 0%
where the time goes in v1:
time: 128 us; the launch traced here: 127 us
  Pallas kernels  119 us (93%)
  local copies, waits for them, and re-layouts  6.85 us (5%)
    pallas_call x1, Pallas kernels, merge_call(): pl.pallas_call(functools.partial(merge_kernel, channels), out_shape=(jax....  77.1 us
    pallas_call x1, Pallas kernels, halo_call(): pl.pallas_call(halo_kernel, out_shape=jax.ShapeDtypeStruct((2, EXT, EXT),...  22.5 us
    pallas_call x1, Pallas kernels, compute_call(): pl.pallas_call(functools.partial(compute_kernel, slots), out_shape=(jax.S...  19.5 us
    unnamed x28, local copies, waits for them, and re-layouts  6.85 us

profile of v1, /device:TPU:1, one launch (start us, length us, event | category | flops | bytes accessed | tf_op | source)
XLA Modules:
  0.0 127.4 jit_solution(2075039380145944779)
XLA Ops:
  0.6 0.1 add_multiply_fusion
  0.7 0.7 broadcast_subtract_fusion.offs
  1.4 1.3 copy-done.1
  2.7 0.0 copy-start.6
  2.7 0.0 copy-start.7
  2.7 0.0 copy-start.8
  2.7 0.0 copy-start.9
  2.7 0.0 copy-start.10
  2.7 0.0 copy-start.11
  2.7 22.5 %halo.1.ext = f32[2,640,640]{2,1,0:T(8,128)S(1)} custom-call(f32[2,384,384]{2,1,0:T(8,128)S(1)} %copy-done.1), custom_call_target="tpu_custom_call" | custom-call | tf_op jit(solution)/shard_map/halo/pallas_call | solution.py:281
  25.2 0.0 copy-start
  25.2 1.7 %copy-done = f32[2,640,640]{2,1,0:T(8,128)} copy-done((f32[2,640,640]{2,1,0:T(8,128)}, f32[2,640,640]{2,1,0:T(8,128)S(1)}, u32[]{:S(2)}) %copy-start) | copy-done | bytes 3276824
  26.9 0.0 copy-done.2
  26.9 0.0 copy-done.3
  26.9 0.0 copy-done.4
  26.9 0.0 copy-done.5
  26.9 0.0 copy-done.6
  27.0 0.0 copy-done.7
  27.0 0.0 copy-done.8
  27.0 0.0 copy-done.9
  27.0 19.5 %positions.1 = (f32[3,640,640]{2,1,0:T(8,128)}, f32[9,256,256]{2,1,0:T(8,128)}) custom-call(s32[2,2]{1,0:T(2,128)S(1)} %broadcast_subtract_fusion.offs, f32[2,640,640]{2,1,0:T(8,128)} %copy-done, f32[4,2,256,256]{3,2,1,0:T(8,128)} %probe.1, f32[2,256,256]{2,1,0:T(8,128)S(1)} %copy-done.2, s32[256,256]{1,0:T(8,128)S(1)} %copy-done.7, ...), custom_call_target="tpu_custom_call" | custom-call | tf_op jit(solution)/shard_map/positions/pallas_call | solution.py:191
  46.5 77.1 %merge.1 = (f32[2,3,16,8,384]{4,3,2,1,0:T(8,128)}, f32[8,4,4,2,8,256]{5,4,3,2,1,0:T(8,128)}) custom-call(f32[15,8,2,8,640]{4,3,2,1,0:T(8,128)} %bitcast.10, f32[9,4,4,2,8,256]{5,4,3,2,1,0:T(8,128)} %bitcast.11, f32[2,3,16,8,384]{4,3,2,1,0:T(8,128)} %bitcast.8, f32[8,4,4,2,8,256]{5,4,3,2,1,0:T(8,128)} %bitcast.9), custom_call_target="tpu_custom_call" | custom-call | tf_op jit(solution)/shard_map/merge/pallas_call | solution.py:575
  123.6 2.5 %copy.17 = f32[2,384,384]{2,1,0:T(8,128)} copy(f32[2,384,384]{2,1,0:T(8,128)} %bitcast.13) | data formatting | bytes 2359296
  126.1 1.3 %copy.18 = f32[4,2,256,256]{3,2,1,0:T(8,128)} copy(f32[4,2,256,256]{3,2,1,0:T(8,128)S(1)} %bitcast.12) | data formatting | bytes 4194304
  (9 shorter events, 0.0 us)
Async XLA Ops:
  1.4 1.3 copy-start.1
  2.7 24.3 %copy-start.2 = (f32[2,256,256]{2,1,0:T(8,128)S(1)}, f32[2,256,256]{2,1,0:T(8,128)}, u32[]{:S(2)}) copy-start(f32[2,256,256]{2,1,0:T(8,128)} %amps.1) | copy-start | bytes 1572868
  2.7 24.3 %copy-start.3 = (bf16[256,768]{1,0:T(8,128)(2,1)S(1)}, bf16[256,768]{1,0:T(8,128)(2,1)}, u32[]{:S(2)}) copy-start(bf16[256,768]{1,0:T(8,128)(2,1)} %constant.28.clone.il) | copy-start | bytes 1179652
  2.7 24.3 %copy-start.4 = (bf16[256,768]{1,0:T(8,128)(2,1)S(1)}, bf16[256,768]{1,0:T(8,128)(2,1)}, u32[]{:S(2)}) copy-start(bf16[256,768]{1,0:T(8,128)(2,1)} %constant.27.clone.fl) | copy-start | bytes 1179652
  2.7 24.3 %copy-start.5 = (bf16[768,256]{1,0:T(8,128)(2,1)S(1)}, bf16[768,256]{1,0:T(8,128)(2,1)}, u32[]{:S(2)}) copy-start(bf16[768,256]{1,0:T(8,128)(2,1)} %constant.26.clone.ir) | copy-start | bytes 1179652
  2.7 24.3 %copy-start.6 = (bf16[768,256]{1,0:T(8,128)(2,1)S(1)}, bf16[768,256]{1,0:T(8,128)(2,1)}, u32[]{:S(2)}) copy-start(bf16[768,256]{1,0:T(8,128)(2,1)} %constant.25.clone.fr) | copy-start | bytes 1179652
  2.7 24.3 %copy-start.7 = (s32[256,256]{1,0:T(8,128)S(1)}, s32[256,256]{1,0:T(8,128)}, u32[]{:S(2)}) copy-start(s32[256,256]{1,0:T(8,128)} %live.1) | copy-start | bytes 786436
  2.7 24.3 %copy-start.8 = (bf16[256,256]{1,0:T(8,128)(2,1)S(1)}, bf16[256,256]{1,0:T(8,128)(2,1)}, u32[]{:S(2)}) copy-start(bf16[256,256]{1,0:T(8,128)(2,1)} %constant.32.clone.pick_t) | copy-start | bytes 393220
  2.7 24.3 %copy-start.9 = (bf16[256,256]{1,0:T(8,128)(2,1)S(1)}, bf16[256,256]{1,0:T(8,128)(2,1)}, u32[]{:S(2)}) copy-start(bf16[256,256]{1,0:T(8,128)(2,1)} %constant.31.clone.pick) | copy-start | bytes 393220
  2.7 24.3 %copy-start.10 = (f32[2,128,128]{2,1,0:T(8,128)S(1)}, f32[2,128,128]{2,1,0:T(8,128)}, u32[]{:S(2)}) copy-start(f32[2,128,128]{2,1,0:T(8,128)} %constant.30.clone.rtw) | copy-start | bytes 393220
  2.7 24.3 %copy-start.11 = (f32[2,8,128]{2,1,0:T(8,128)S(1)}, f32[2,8,128]{2,1,0:T(8,128)}, u32[]{:S(2)}) copy-start(f32[2,8,128]{2,1,0:T(8,128)} %constant.29.clone.ltw) | copy-start | bytes 24580
  25.2 1.7 %copy-start = (f32[2,640,640]{2,1,0:T(8,128)}, f32[2,640,640]{2,1,0:T(8,128)S(1)}, u32[]{:S(2)}) copy-start(f32[2,640,640]{2,1,0:T(8,128)S(1)} %halo.1.ext) | copy-start | bytes 9830404
  123.5 2.5 %copy-start.12 = (f32[8,4,4,2,8,256]{5,4,3,2,1,0:T(8,128)S(1)}, f32[8,4,4,2,8,256]{5,4,3,2,1,0:T(8,128)}, u32[]{:S(2)}) copy-start(f32[8,4,4,2,8,256]{5,4,3,2,1,0:T(8,128)} %get-tuple-element.9) | copy-start | bytes 6291460

commit v2 on v1

--- a/solution.py
+++ b/solution.py
@@ -24,25 +24,29 @@
     m = np.block([[c, -s], [s, c]]).astype(np.float32)
     hi = m.astype(ml_dtypes.bfloat16)
     lo = (m - hi.astype(np.float32)).astype(ml_dtypes.bfloat16)
-    fwd_right = np.concatenate([hi, hi, lo], 0)
-    inv_right = np.concatenate([hi.T, hi.T, lo.T], 0)
-    fwd_left = np.concatenate([hi.T, hi.T, lo.T], 1)
-    inv_left = np.concatenate([hi, hi, lo], 1)
     th = 2.0 * np.pi * k / N
     tw = np.stack([np.cos(th), np.sin(th)]).astype(np.float32)
-    lane_tw = np.stack([np.tile(tw[0], (8, 1)), np.tile(tw[1], (8, 1))])
-    row_tw = np.stack([np.tile(tw[0][:, None], (1, H)), np.tile(tw[1][:, None], (1, H))])
+    turns = np.stack([np.tile(tw[0][:, None], (1, H)), np.tile(tw[1][:, None], (1, H)),
+                      np.tile(tw[0], (H, 1)), np.tile(tw[1], (H, 1))])
     perm = np.concatenate([np.arange(0, N, 2), np.arange(1, N, 2)])
     pick = np.zeros((N, N), np.float32)
     pick[np.arange(N), perm] = 1.0
     pick = pick.astype(ml_dtypes.bfloat16)
-    return fwd_right, inv_right, fwd_left, inv_left, lane_tw, row_tw, pick, pick.T.copy()
+    return np.stack([hi, lo, hi.T, lo.T, pick, pick.T]), turns
 
 
 def split(x):
     hi = x.astype(bf16)
     lo = (x - hi.astype(f32)).astype(bf16)
     return hi, lo
+
+
+def over(hi, lo):
+    return jnp.concatenate([hi, hi, lo], 0)
+
+
+def beside(hi, lo):
+    return jnp.concatenate([hi, hi, lo], 1)
 
 
 def right(x, table):
@@ -89,31 +93,74 @@
     return jnp.concatenate([jnp.where(keep, t[0], 0.0), jnp.where(keep, t[1], t[0]), jnp.where(keep, 0.0, t[1])], 1)
 
 
-def compute_kernel(slots, offs, ext, probe, amps, live, fr, ir, fl, il, ltw, rtw, pick, pick_t,
-                   frame, sums,
-                   patch, far, fac, grad, weight, mask):
+STRIDES = ((32, 64), (16, 48), (8, 40), (4, 36), (2, 34), (1, 33))
+
+
+def bit_of(x, bit):
+    return lax.rem(lax.div(x, bit), 2) == 1
+
+
+def cut_window(ext, c, row, col):
+    row8, u = lax.div(row, 8), lax.div(col, 128)
+    blocks = [ext[c, :, 128 * i:128 * (i + 1)].reshape(EXT // 8, 8, 128) for i in range(5)]
+    out = []
+    for o in range(3):
+        v = jnp.where(u == 0, blocks[o], jnp.where(u == 1, blocks[o + 1], blocks[o + 2]))
+        for bit, size in STRIDES:
+            if bit == 32:
+                v = jnp.concatenate([jnp.where(bit_of(row8, bit), v[32:80], v[0:48]), v[48:64]], 0)
+            else:
+                v = jnp.where(bit_of(row8, bit), v[bit:bit + size], v[:size])
+        out.append(v.reshape(N + 8, 128))
+    return shift_up_left(jnp.concatenate(out, 1), row - 8 * row8, col - 128 * u)
+
+
+def add_window(frame, c, x, row, col):
+    row8, u = lax.div(row, 8), lax.div(col, 128)
+    moved = shift_down_right(x, row - 8 * row8, col - 128 * u)
+    placed = []
+    for o in range(3):
+        v = moved[:, 128 * o:128 * (o + 1)].reshape(N // 8 + 1, 8, 128)
+        for bit in (1, 2, 4, 8, 16):
+            none = jnp.zeros((bit, 8, 128), f32)
+            v = jnp.where(bit_of(row8, bit), jnp.concatenate([none, v], 0), jnp.concatenate([v, none], 0))
+        none = jnp.zeros((32, 8, 128), f32)
+        v = jnp.where(bit_of(row8, 32), jnp.concatenate([none, v[:48]], 0), jnp.concatenate([v, none[:16]], 0))
+        placed.append(v)
+    none = jnp.zeros((EXT // 8, 8, 128), f32)
+
+    def at(k):
+        return placed[k] if 0 <= k < 3 else none
+
+    for o in range(5):
+        v = jnp.where(u == 0, at(o), jnp.where(u == 1, at(o - 1), at(o - 2)))
+        frame[5 * c:5 * c + 5, :, :, :, 128 * o:128 * (o + 1)] += v.reshape(5, *frame.shape[1:4], 128)
+
+
+def prepare(live, probe, squares, mask, wparts):
+    power = jnp.zeros((N, N), f32)
+    for m in range(probe.shape[0]):
+        power = power + (probe[m, 0] * probe[m, 0] + probe[m, 1] * probe[m, 1])
+    for i in range(3):
+        wparts[i] = power.astype(bf16)
+        power = power - wparts[i].astype(f32)
+    on = (live[...] == 1).astype(bf16)
+    on = jnp.dot(squares[4], on, preferred_element_type=f32).astype(bf16)
+    mask[...] = jnp.dot(on, squares[5], preferred_element_type=f32)
+
+
+def visit_positions(slots, offs, ext, probe, amps, squares, turns, frame, sums, patch, far, fac, grad, mask):
     modes = probe.shape[0]
-    frame[...] = jnp.zeros_like(frame)
-    sums[...] = jnp.zeros_like(sums)
-    w = jnp.zeros((N, N), f32)
-    for m in range(modes):
-        w = w + (probe[m, 0] * probe[m, 0] + probe[m, 1] * probe[m, 1])
-    weight[...] = w
-    on = (live[...] == 1).astype(bf16)
-    on = jnp.dot(pick[...], on, preferred_element_type=f32).astype(bf16)
-    mask[...] = jnp.dot(on, pick_t[...], preferred_element_type=f32)
+    split_rows = sums.shape[1:]
 
     @pl.loop(0, slots)
     def _(p):
-        row, col = offs[p, 0], offs[p, 1]
-        row8, col128 = row // 8, col // 128
-        srow, scol = row - row8 * 8, col - col128 * 128
-        rows = pl.ds(pl.multiple_of(row8 * 8, 8), N + 8)
-        cols = pl.ds(pl.multiple_of(col128 * 128, 128), N + 128)
+        row = offs[p, 0] - TILE * lax.axis_index("ty")
+        col = offs[p, 1] - TILE * lax.axis_index("tx")
         for c in range(2):
-            patch[c] = shift_up_left(ext[c, rows, cols], srow, scol)
+            patch[c] = cut_window(ext, c, row, col)
         pr, pi = patch[0], patch[1]
-        sums[2 * modes] += pr * pr + pi * pi
+        sums[2 * modes] += (pr * pr + pi * pi).reshape(split_rows)
         grad[...] = jnp.zeros_like(grad)
         fac[...] = jnp.zeros_like(fac)
 
@@ -125,25 +172,25 @@
             wi = qr * pi + qi * pr
             ar, ai = wr[:, :H] + wr[:, H:], wi[:, :H] + wi[:, H:]
             br, bi = wr[:, :H] - wr[:, H:], wi[:, :H] - wi[:, H:]
-            tc, ts = ltw[0, 0:1], ltw[1, 0:1]
+            tc, ts = turns[2, 0:1], turns[3, 0:1]
             br, bi = br * tc + bi * ts, bi * tc - br * ts
-            even = right(jnp.concatenate([ar, ai], 1), fr[...])
-            odd = right(jnp.concatenate([br, bi], 1), fr[...])
+            even = right(jnp.concatenate([ar, ai], 1), over(squares[0], squares[1]))
+            odd = right(jnp.concatenate([br, bi], 1), over(squares[0], squares[1]))
             total = None
-            rc, rs = rtw[0], rtw[1]
+            rc, rs = turns[0], turns[1]
             for h, z in enumerate((even, odd)):
                 zr, zi = z[:, :H], z[:, H:]
                 ar, ai = zr[:H] + zr[H:], zi[:H] + zi[H:]
                 br, bi = zr[:H] - zr[H:], zi[:H] - zi[H:]
                 br, bi = br * rc + bi * rs, bi * rc - br * rs
                 both = jnp.concatenate([jnp.concatenate([ar, br], 1), jnp.concatenate([ai, bi], 1)], 0)
-                out = left(fl[...], both)
+                out = left(beside(squares[2], squares[3]), both)
                 far[m, h] = out
                 sq = out * out
                 power = sq[:H] + sq[H:]
                 fac[h] += power
 
-        amp = split_dot_r(split_dot_l(pick[...], amps[p]), pick_t[...])
+        amp = split_dot_r(split_dot_l(squares[4], amps[p]), squares[5])
         for h in range(2):
             want = jnp.concatenate([amp[:H, h * H:(h + 1) * H], amp[H:, h * H:(h + 1) * H]], 1)
             lv = jnp.concatenate([mask[:H, h * H:(h + 1) * H], mask[H:, h * H:(h + 1) * H]], 1)
@@ -151,22 +198,22 @@
 
         @pl.loop(0, modes, unroll=4)
         def _(m):
-            rc, rs = rtw[0], rtw[1]
+            rc, rs = turns[0], turns[1]
             halves = []
             for h in range(2):
                 f = far[m, h]
                 k = fac[h]
                 y = jnp.concatenate([f[:H] * k, f[H:] * k], 0)
-                x = left(il[...], y)
+                x = left(beside(squares[0], squares[1]), y)
                 er, orr = x[:H, :H], x[:H, H:]
                 ei, oi = x[H:, :H], x[H:, H:]
                 orr, oi = orr * rc - oi * rs, oi * rc + orr * rs
                 top = jnp.concatenate([er + orr, ei + oi], 1)
                 bottom = jnp.concatenate([er - orr, ei - oi], 1)
-                halves.append(right(jnp.concatenate([top, bottom], 0), ir[...]))
+                halves.append(right(jnp.concatenate([top, bottom], 0), over(squares[2], squares[3])))
             e, o = halves
             er, ei, orr, oi = e[:, :H], e[:, H:], o[:, :H], o[:, H:]
-            tc, ts = ltw[0, 0:1], ltw[1, 0:1]
+            tc, ts = turns[2, 0:1], turns[3, 0:1]
             orr, oi = orr * tc - oi * ts, oi * tc + orr * ts
             nr = jnp.concatenate([er + orr, er - orr], 1)
             ni = jnp.concatenate([ei + oi, ei - oi], 1)
@@ -176,37 +223,11 @@
             di = ni - (qr * pi + qi * pr)
             grad[0] += qr * dr + qi * di
             grad[1] += qr * di - qi * dr
-            sums[2 * m] += pr * dr + pi * di
-            sums[2 * m + 1] += pr * di - pi * dr
-
-        for c in range(frame.shape[0]):
-            frame[c, rows, cols] += shift_down_right(grad[c] if c < 2 else weight[...], srow, scol)
-
-
-def compute_call(offs, ext, probe, amps, live, channels=3):
-    slots = amps.shape[0]
-    modes = probe.shape[0]
-    vm = pl.BlockSpec(memory_space=pltpu.VMEM)
-    consts = [jnp.asarray(t) for t in tables()]
-    return pl.pallas_call(
-        functools.partial(compute_kernel, slots),
-        out_shape=(
-            jax.ShapeDtypeStruct((channels, EXT, EXT), f32),
-            jax.ShapeDtypeStruct((2 * modes + 1, N, N), f32),
-        ),
-        in_specs=[pl.BlockSpec(memory_space=pltpu.SMEM)] + [vm] * (4 + len(consts)),
-        out_specs=(vm, vm),
-        scratch_shapes=[
-            pltpu.VMEM((2, N, N), f32),
-            pltpu.VMEM((modes, 2, N, N), f32),
-            pltpu.VMEM((2, H, N), f32),
-            pltpu.VMEM((2, N, N), f32),
-            pltpu.VMEM((N, N), f32),
-            pltpu.VMEM((N, N), f32),
-        ],
-        compiler_params=pltpu.CompilerParams(vmem_limit_bytes=50 * 2**20),
-        name="positions",
-    )(offs, ext, probe, amps, live, *consts)
+            sums[2 * m] += (pr * dr + pi * di).reshape(split_rows)
+            sums[2 * m + 1] += (pr * di - pi * dr).reshape(split_rows)
+
+        for c in range(2):
+            add_window(frame, c, grad[c], row, col)
 
 
 MESH = pl.DeviceIdType.MESH
@@ -248,51 +269,88 @@
     return p, p // 2, lax.rem(p, 2), lax.axis_index("ty"), lax.axis_index("tx")
 
 
-def halo_kernel(obj, ext, here, send, recv):
+SHARED = 4
+
+
+def gather_halo(w, offs, obj, ext, table, here, ready):
     p, z, c, a, b = places()
+    nz = N_POS // 2
     tile = obj.shape[1]
     up, down = lax.rem(a + N_Y - 1, N_Y), lax.rem(a + 1, N_Y)
     left, right_ = lax.rem(b + N_X - 1, N_X), lax.rem(b + 1, N_X)
+    after, before = {"pos": 2 * lax.rem(z + 1, nz) + c}, {"pos": 2 * lax.rem(z + nz - 1, nz) + c}
     sib = {"pos": 2 * z + 1 - c}
-    greet([sib, {"tx": left}, {"tx": right_}, {"ty": up}, {"ty": down},
-           {"ty": up, "tx": left}, {"ty": down, "tx": right_}])
-    w = Wires(send, recv)
+    odd = lax.rem(z, 2)
+    group = [{"pos": lax.rem(p + k, N_POS)} for k in range(1, N_POS)]
     own = pltpu.make_async_copy(obj, ext.at[:, 0:tile, 0:tile], here)
     own.start()
-    parts = [
-        (obj.at[c, 0:N, 0:N], (pl.ds(tile, N), pl.ds(tile, N)), {"ty": up, "tx": left}),
-        (obj.at[c, :, 0:N], (pl.ds(0, tile), pl.ds(tile, N)), {"tx": left}),
-        (obj.at[c, 0:N, :], (pl.ds(tile, N), pl.ds(0, tile)), {"ty": up}),
-    ]
-    got = []
-    for src, (rows, cols), to in parts:
-        got.append(w.start(src, ext.at[c, rows, cols], w.slot(), to))
-    shared = []
-    for made, (src, (rows, cols), to) in list(zip(got, parts)):
-        made.wait_recv()
-        shared.append(w.start(ext.at[c, rows, cols], ext.at[c, rows, cols], w.slot(), sib))
-    for made in shared:
+
+    def spans(e, k):
+        if k == SHARED:
+            return pl.ds(256, 128), pl.ds(192, 64)
+        return (pl.ds(pl.multiple_of(128 * e + 32 * k, 8), 32), pl.ds(pl.multiple_of(96 * e + 24 * k, 8), 24))
+
+    def lower(rows):
+        return pl.ds(pl.multiple_of(tile + rows.start, 8), rows.size)
+
+    def rims(e, k):
+        side, below = spans(e, k)
+        return ext.at[c, side, tile:tile + N], ext.at[c, lower(below), :]
+
+    came = []
+    for k in range(SHARED + 1):
+        side, below = spans(odd, k)
+        came.append((
+            w.start(obj.at[c, side, 0:N], ext.at[c, side, tile:tile + N], w.slot(), {"tx": left}),
+            w.start(obj.at[c, below, :], ext.at[c, lower(below), 0:tile], w.slot(), {"ty": up}),
+            w.start(obj.at[c, below, 0:N], ext.at[c, lower(below), tile:tile + N], w.slot(), {"ty": up, "tx": left}),
+        ))
+    lane = lax.broadcasted_iota(jnp.int32, (1, 128), 1)
+    row = jnp.zeros((1, 128), jnp.int32)
+    for i in range(2 * offs.shape[0]):
+        row = jnp.where(lane == i, offs[i // 2, i % 2], row)
+    table[0, p] = row
+    line = table.at[0, p]
+    lines = [w.start(line, line, w.slot(), to) for to in group]
+    ready()
+    pair, relay = [], []
+    for k in range(SHARED + 1):
+        for made in came[k]:
+            made.wait_recv()
+        for spot in rims(odd, k):
+            if k < SHARED:
+                relay.append(w.start(spot, spot, w.slot(), after if k % 2 == 0 else before))
+        for spot in rims(odd, k):
+            pair.append(w.start(spot, spot, w.slot(), sib))
+        if k == 1:
+            for made in lines:
+                made.wait_recv()
+            for t, to in ((1, {"ty": down}), (2, {"tx": right_}), (3, {"ty": down, "tx": right_})):
+                pair.append(w.start(table.at[0], table.at[t], w.slot(), to))
+    for k in range(SHARED):
+        for i, spot in enumerate(rims(1 - odd, k)):
+            relay[2 * k + i].wait_recv()
+            pair.append(w.start(spot, spot, w.slot(), sib))
+    for made in pair:
         made.wait_recv()
     own.wait()
-    w.finish()
-
-
-def halo_call(obj):
-    return pl.pallas_call(
-        halo_kernel,
-        out_shape=jax.ShapeDtypeStruct((2, EXT, EXT), f32),
-        in_specs=[pl.BlockSpec(memory_space=pltpu.VMEM)],
-        out_specs=pl.BlockSpec(memory_space=pltpu.VMEM),
-        scratch_shapes=[pltpu.SemaphoreType.DMA, pltpu.SemaphoreType.DMA((6,)), pltpu.SemaphoreType.DMA((6,))],
-        compiler_params=pltpu.CompilerParams(collective_id=0, has_side_effects=True, vmem_limit_bytes=32 * 2**20),
-        name="halo",
-    )(obj)
-
-
-def merge_kernel(channels, frame, sums, obj, probe, out, pout,
-                 s, rin, lin, t, fr, fb, fc, acc, wide, hl, hr, tops, bots, up_in, up_edge, dn_in, dn_edge,
-                 r0, pa, q, pb, tt, st, pz, send, recv):
+
+
+def step_kernel(offs, obj_far, probe_far, amps_far, live_far, squares_far, turns_far, out, pout,
+                ext, table, offs_all, whole_probe, amps, live, squares, turns, patch, far, fac, grad, mask,
+                frame, sums, obj, probe, wparts, hot, rows_of, wsum,
+                s, rin, lin, t, fr, fb, fc, acc, wide, hl, hr, tops, bots, up_in, up_edge, dn_in, dn_edge,
+                r0, pa, q, pb, tt, st, pz, here, send, recv):
+    channels = 2
     p, z, c, a, b = places()
+    lanes = pl.ds(pl.multiple_of(c * 128, 128), 128)
+    others = pl.ds(pl.multiple_of((1 - c) * 128, 128), 128)
+    loads = [pltpu.make_async_copy(src, dst, here.at[i]) for i, (src, dst) in enumerate((
+        (obj_far.at[:, :, p], obj), (probe_far.at[z, a, b, :, :, lanes], probe),
+        (probe_far.reshape(whole_probe.shape), whole_probe), (squares_far, squares), (turns_far, turns),
+        (live_far, live), (amps_far, amps)))]
+    for load in loads:
+        load.start()
     nz = N_POS // 2
     half = nz // 2
     up, down = lax.rem(a + N_Y - 1, N_Y), lax.rem(a + 1, N_Y)
@@ -306,15 +364,62 @@
         return {"pos": 2 * zat(k) + c}
 
     sib = {"pos": 2 * z + 1 - c}
-    greet([sib] + [zdev(k) for k in range(1, nz)]
-          + [{"ty": lax.rem(a + k, N_Y)} for k in range(1, N_Y)]
+    up_edge[...] = jnp.zeros_like(up_edge)
+    dn_edge[...] = jnp.zeros_like(dn_edge)
+    greet([{"ty": lax.rem(a + k, N_Y)} for k in range(1, N_Y)]
           + [{"tx": lax.rem(b + k, N_X)} for k in range(1, N_X)]
           + [{"ty": down, "tx": right_}, {"ty": up, "tx": left}]
-          + [{"pos": following}, {"pos": previous}]
+          + [{"pos": lax.rem(p + k, N_POS)} for k in range(1, N_POS)]
           + [{"pos": N_POS - 1 - p, "ty": down}, {"pos": N_POS - 1 - p, "ty": up}])
     w = Wires(send, recv)
-    up_edge[...] = jnp.zeros_like(up_edge)
-    dn_edge[...] = jnp.zeros_like(dn_edge)
+
+    def ready():
+        for ref in (frame, sums, wsum):
+            ref[...] = jnp.zeros_like(ref)
+        for load in loads[2:]:
+            load.wait()
+        prepare(live, whole_probe, squares, mask, wparts)
+
+    gather_halo(w, offs, obj_far.reshape(2, TILE, TILE), ext, table, here.at[7], ready)
+    known = pltpu.make_async_copy(table, offs_all, here.at[8])
+    known.start()
+    visit_positions(amps.shape[0], offs, ext, whole_probe, amps, squares, turns, frame, sums,
+                    patch, far, fac, grad, mask)
+    known.wait()
+    spread = lax.broadcasted_iota(jnp.int32, (8, N), 1) - lax.broadcasted_iota(jnp.int32, (8, N), 0)
+    lane = lax.broadcasted_iota(jnp.int32, (24, 128), 1)
+
+    def weigh(which):
+        @pl.loop(0, 2 * N_POS)
+        def _(i):
+            row = offs_all[which, lax.div(i, 2), 0, 2 * lax.rem(i, 2)] - TILE * a
+            for g in range(3):
+                first = (g * N_POS + p) * 8 - row
+                hot[pl.ds(pl.multiple_of(24 * i + 8 * g, 8), 8), :] = jnp.where(spread == first, 1.0, 0.0)
+
+        pick = hot[...].astype(bf16)
+        rows_of[...] = (jnp.dot(pick, wparts[0], preferred_element_type=f32)
+                        + jnp.dot(pick, wparts[1], preferred_element_type=f32)
+                        + jnp.dot(pick, wparts[2], preferred_element_type=f32))
+
+        def one(i, carry):
+            col = offs_all[which, lax.div(i, 2), 0, 2 * lax.rem(i, 2) + 1] - TILE * b
+            col = jnp.clip(col + TILE, 0, 2 * TILE)
+            u = lax.div(col, 128)
+            s_ = col - 128 * u
+            u = u - 3
+            x = rows_of[pl.ds(pl.multiple_of(24 * i, 8), 24), :]
+            t0, t1 = pltpu.roll(x[:, :128], s_, 1), pltpu.roll(x[:, 128:], s_, 1)
+            keep = lane >= s_
+            g0, g1, g2 = jnp.where(keep, t0, 0.0), jnp.where(keep, t1, t0), jnp.where(keep, 0.0, t1)
+            return tuple(
+                carry[o] + jnp.where(u == o, g0, jnp.where(u == o - 1, g1, jnp.where(u == o - 2, g2, 0.0)))
+                for o in range(3))
+
+        zero = jnp.zeros((24, 128), f32)
+        added = lax.fori_loop(0, 2 * N_POS, one, (zero,) * 3, unroll=4)
+        wsum[...] += jnp.concatenate(added, 1)
+
     total = frame.shape[0]
     cut = (total + 1) // 2
     parts = (pl.ds(0, cut), pl.ds(cut, total - cut))
@@ -346,6 +451,7 @@
                         s[d, parts[part]] += box[step - 1, parts[part]]
                     went[step, way, part] = w.start(
                         s.at[d, parts[part]], box.at[step, parts[part]], w.slot(), zdev(way))
+            weigh(step)
             yield
         mine(0)
         last = half - 1
@@ -365,9 +471,10 @@
         acc[:, 0:2] += fb[...]
         f3.wait_recv()
         acc[:, 0:2, :, 0:N] += fc[...]
-        share = acc[2] + 1.0
+        share = wsum[...].reshape(3, 8, TILE) + 1.0
+        loads[0].wait()
         for ch in range(2):
-            wide[ch, :, :, 128:128 + TILE] = obj[ch, :, p] + acc[ch] / share
+            wide[ch, :, :, 128:128 + TILE] = obj[ch] + acc[ch] / share
         h1 = w.start(wide.at[:, :, :, TILE:TILE + 128], hl, w.slot(), {"tx": right_})
         h2 = w.start(wide.at[:, :, :, 128:256], hr, w.slot(), {"tx": left})
         yield
@@ -472,9 +579,6 @@
             made.wait_recv()
         yield
 
-    lanes = pl.ds(pl.multiple_of(c * 128, 128), 128)
-    others = pl.ds(pl.multiple_of((1 - c) * 128, 128), 128)
-
     def at_y(k):
         return lax.rem(a + (k + N_Y), N_Y)
 
@@ -517,7 +621,8 @@
         for k in range(1, nz):
             third[k - 1].wait_recv()
             whole = whole + pz[k - 1]
-        pout[z, a, b, :, :, lanes] = probe[z, a, b, :, :, lanes] + whole[0] / (whole[1] + 1.0)
+        loads[1].wait()
+        pout[z, a, b, :, :, lanes] = probe[...] + whole[0] / (whole[1] + 1.0)
         spot = pout.at[z, a, b, :, :, lanes]
         fourth = [w.start(spot, spot, w.slot(), zdev(k)) for k in range(1, nz)]
         yield
@@ -559,48 +664,53 @@
 
 
 MERGE_ORDER = "opo" + "po" + "opo" + "pop" + "opopo" + "oo"
-MERGE_WIRES = 110
-
-
-def merge_call(frame, sums, obj, probe):
-    channels = frame.shape[0]
+WIRES = 170
+
+
+def step_call(offs, obj, probe, amps, live):
+    channels = 2
     vm = pl.BlockSpec(memory_space=pltpu.VMEM)
+    far = pl.BlockSpec(memory_space=pl.ANY)
     nz = N_POS // 2
     g = 5 * channels
     half = nz // 2
+    modes = probe.shape[0]
+    consts = [jnp.asarray(x) for x in tables()]
 
     def v(*shape):
         return pltpu.VMEM(shape, f32)
 
     out, pout = pl.pallas_call(
-        functools.partial(merge_kernel, channels),
+        step_kernel,
         out_shape=(
             jax.ShapeDtypeStruct((2, 3, N_POS, 8, TILE), f32),
             jax.ShapeDtypeStruct((8, N_Y, N_X, 2, 8, N), f32),
         ),
-        in_specs=[vm] * 4,
+        in_specs=[pl.BlockSpec(memory_space=pltpu.SMEM)] + [far] * 6,
         out_specs=(vm, vm),
         scratch_shapes=[
+            v(2, EXT, EXT), pltpu.VMEM((4, N_POS, 1, 128), jnp.int32), pltpu.SMEM((4, N_POS, 1, 128), jnp.int32),
+            v(*probe.shape), v(*amps.shape), pltpu.VMEM((N, N), jnp.int32), pltpu.VMEM((6, N, N), bf16), v(4, H, H),
+            v(2, N, N), v(modes, 2, N, N), v(2, H, N), v(2, N, N), v(N, N),
+            v(g, nz, 2, 8, EXT), v(9, N_Y, N_X, 2, 8, N),
+            v(2, 3, 8, TILE), v(2, 8, 128), pltpu.VMEM((3, N, N), bf16),
+            v(48 * N_POS, N), v(48 * N_POS, N), v(24, TILE),
             v(nz, g, 8, EXT), v(half, g, 8, EXT), v(half, g, 8, EXT), v(channels, 5, 8, EXT),
             v(channels, 3, 8, N), v(channels, 2, 8, TILE), v(channels, 2, 8, N), v(channels, 3, 8, TILE),
             v(2, 3, 8, EXT), v(2, 3, 8, 128), v(2, 3, 8, 128),
             v(8, EXT), v(8, EXT), v(8, EXT), v(8, EXT), v(8, EXT), v(8, EXT),
             v(9, N_Y, N_X, 2, 8, 128), v(2, 3, 9, 4, 8, 128), v(2, 9, 4, 8, 128), v(2, 3, 9, 8, 128),
             v(9, 2, 8, 128), v(8, 2, 2, 8, 128), v(7, 2, 2, 8, 128),
-            pltpu.SemaphoreType.DMA((MERGE_WIRES,)), pltpu.SemaphoreType.DMA((MERGE_WIRES,)),
+            pltpu.SemaphoreType.DMA((9,)), pltpu.SemaphoreType.DMA((WIRES,)), pltpu.SemaphoreType.DMA((WIRES,)),
         ],
-        compiler_params=pltpu.CompilerParams(collective_id=1, has_side_effects=True, vmem_limit_bytes=56 * 2**20),
-        name="merge",
-    )(frame.reshape(g, nz, 2, 8, EXT), sums.reshape(9, N_Y, N_X, 2, 8, N),
-      obj.reshape(2, 3, N_POS, 8, TILE), probe.reshape(8, N_Y, N_X, 2, 8, N))
+        compiler_params=pltpu.CompilerParams(collective_id=0, has_side_effects=True, vmem_limit_bytes=60 * 2**20),
+        name="step",
+    )(offs, obj.reshape(2, 3, N_POS, 8, TILE), probe.reshape(8, N_Y, N_X, 2, 8, N), amps, live, *consts)
     return out.reshape(2, TILE, TILE), pout.reshape(probe.shape)
 
 
 def body(object_field, probe, amplitudes, live_pixels, offsets):
-    base = jnp.stack([lax.axis_index("ty"), lax.axis_index("tx")]).astype(jnp.int32) * TILE
-    ext = halo_call(object_field)
-    frame, sums = compute_call(offsets - base, ext, probe, amplitudes, live_pixels)
-    return merge_call(frame, sums, object_field, probe)
+    return step_call(offsets, object_field, probe, amplitudes, live_pixels)
 
 
 def solution(mesh):

time: 128 us -> 101 us (0.79)
  Pallas kernels: 119 us -> 96.9 us
  local copies, waits for them, and re-layouts: 6.85 us -> 3.83 us
    pallas_call x3 -> x1, Pallas kernels: 119 us -> 96.9 us  [step_call(): pl.pallas_call(step_kernel, out_shape=(jax.ShapeDtypeStruct((2, 3, N_POS,...]
    unnamed x28 -> x4, local copies, waits for them, and re-layouts: 6.85 us -> 3.83 us
where the time goes in v2:
time: 101 us
  Pallas kernels  96.9 us (96%)
  local copies, waits for them, and re-layouts  3.83 us (4%)
    pallas_call x1, Pallas kernels, step_call(): pl.pallas_call(step_kernel, out_shape=(jax.ShapeDtypeStruct((2, 3, N_POS,...  96.9 us
    unnamed x4, local copies, waits for them, and re-layouts  3.83 us

profile of v2, /device:TPU:1, one launch (start us, length us, event | category | flops | bytes accessed | tf_op | source)
XLA Modules:
  0.0 101.4 jit_solution(15025222955528719050)
XLA Ops:
  0.6 96.9 %step.1 = (f32[2,3,16,8,384]{4,3,2,1,0:T(8,128)}, f32[8,4,4,2,8,256]{5,4,3,2,1,0:T(8,128)}) custom-call(s32[2,2]{1,0:T(2,128)} %offs.1, f32[2,3,16,8,384]{4,3,2,1,0:T(8,128)} %bitcast.7, f32[8,4,4,2,8,256]{5,4,3,2,1,0:T(8,128)} %bitcast.4, f32[2,256,256]{2,1,0:T(8,128)} %amps_far.1, s32[256,256]{1,0:T(8,128)} %live_far.1, ...), custom_call_target="tpu_custom_call" | custom-call | tf_op jit(solution)/shard_map/step/pallas_call | solution.py:683
  97.5 0.0 copy-start
  97.5 2.5 %copy.11 = f32[2,384,384]{2,1,0:T(8,128)} copy(f32[2,384,384]{2,1,0:T(8,128)} %bitcast.6) | data formatting | bytes 2359296
  100.0 0.0 copy-done
  100.0 1.3 %copy.12 = f32[4,2,256,256]{3,2,1,0:T(8,128)} copy(f32[4,2,256,256]{3,2,1,0:T(8,128)S(1)} %bitcast.5) | data formatting | bytes 4194304
Async XLA Ops:
  97.5 2.5 %copy-start = (f32[8,4,4,2,8,256]{5,4,3,2,1,0:T(8,128)S(1)}, f32[8,4,4,2,8,256]{5,4,3,2,1,0:T(8,128)}, u32[]{:S(2)}) copy-start(f32[8,4,4,2,8,256]{5,4,3,2,1,0:T(8,128)} %get-tuple-element.5) | copy-start | bytes 6291460

commit v3 on v2

--- a/solution.py
+++ b/solution.py
@@ -149,7 +149,7 @@
     mask[...] = jnp.dot(on, squares[5], preferred_element_type=f32)
 
 
-def visit_positions(slots, offs, ext, probe, amps, squares, turns, frame, sums, patch, far, fac, grad, mask):
+def visit_positions(slots, offs, ext, probe, amps, squares, turns, frame, sums, patch, far, fac, grad, mask, hand_over):
     modes = probe.shape[0]
     split_rows = sums.shape[1:]
 
@@ -161,6 +161,11 @@
             patch[c] = cut_window(ext, c, row, col)
         pr, pi = patch[0], patch[1]
         sums[2 * modes] += (pr * pr + pi * pi).reshape(split_rows)
+
+        @pl.when(p == slots - 1)
+        def _():
+            hand_over(modes)
+
         grad[...] = jnp.zeros_like(grad)
         fac[...] = jnp.zeros_like(fac)
 
@@ -196,8 +201,7 @@
             lv = jnp.concatenate([mask[:H, h * H:(h + 1) * H], mask[H:, h * H:(h + 1) * H]], 1)
             fac[h] = jnp.where(lv > 0.5, want * lax.rsqrt(jnp.maximum(fac[h], intensity_floor)), 1.0)
 
-        @pl.loop(0, modes, unroll=4)
-        def _(m):
+        for m in range(modes):
             rc, rs = turns[0], turns[1]
             halves = []
             for h in range(2):
@@ -226,6 +230,10 @@
             sums[2 * m] += (pr * dr + pi * di).reshape(split_rows)
             sums[2 * m + 1] += (pr * di - pi * dr).reshape(split_rows)
 
+            @pl.when(p == slots - 1)
+            def _():
+                hand_over(m)
+
         for c in range(2):
             add_window(frame, c, grad[c], row, col)
 
@@ -298,13 +306,18 @@
         return ext.at[c, side, tile:tile + N], ext.at[c, lower(below), :]
 
     came = []
-    for k in range(SHARED + 1):
+
+    def push(k):
         side, below = spans(odd, k)
         came.append((
             w.start(obj.at[c, side, 0:N], ext.at[c, side, tile:tile + N], w.slot(), {"tx": left}),
             w.start(obj.at[c, below, :], ext.at[c, lower(below), 0:tile], w.slot(), {"ty": up}),
             w.start(obj.at[c, below, 0:N], ext.at[c, lower(below), tile:tile + N], w.slot(), {"ty": up, "tx": left}),
         ))
+
+    push(0)
+    for k in range(1, SHARED):
+        push(k)
     lane = lax.broadcasted_iota(jnp.int32, (1, 128), 1)
     row = jnp.zeros((1, 128), jnp.int32)
     for i in range(2 * offs.shape[0]):
@@ -317,6 +330,8 @@
     for k in range(SHARED + 1):
         for made in came[k]:
             made.wait_recv()
+        if k == 1:
+            push(SHARED)
         for spot in rims(odd, k):
             if k < SHARED:
                 relay.append(w.start(spot, spot, w.slot(), after if k % 2 == 0 else before))
@@ -364,13 +379,15 @@
         return {"pos": 2 * zat(k) + c}
 
     sib = {"pos": 2 * z + 1 - c}
-    up_edge[...] = jnp.zeros_like(up_edge)
-    dn_edge[...] = jnp.zeros_like(dn_edge)
+    for ref in (tops, bots, up_in, up_edge, dn_in, dn_edge):
+        ref[...] = jnp.zeros_like(ref)
     greet([{"ty": lax.rem(a + k, N_Y)} for k in range(1, N_Y)]
           + [{"tx": lax.rem(b + k, N_X)} for k in range(1, N_X)]
           + [{"ty": down, "tx": right_}, {"ty": up, "tx": left}]
           + [{"pos": lax.rem(p + k, N_POS)} for k in range(1, N_POS)]
-          + [{"pos": N_POS - 1 - p, "ty": down}, {"pos": N_POS - 1 - p, "ty": up}])
+          + [{"pos": N_POS - 1 - p, "ty": down}, {"pos": N_POS - 1 - p, "ty": up}]
+          + [{"pos": N_POS - 1 - p, "ty": down, "tx": left}, {"pos": N_POS - 1 - p, "ty": up, "tx": right_}]
+          + [{"pos": following, "tx": left}, {"pos": previous, "tx": right_}])
     w = Wires(send, recv)
 
     def ready():
@@ -381,10 +398,16 @@
         prepare(live, whole_probe, squares, mask, wparts)
 
     gather_halo(w, offs, obj_far.reshape(2, TILE, TILE), ext, table, here.at[7], ready)
+    swap_slots = [w.slot() for _ in range(whole_probe.shape[0] + 1)]
+
+    def swap(m):
+        two = pl.ds(2 * m, 2 if m < whole_probe.shape[0] else 1)
+        return w.copy(sums.at[two, :, :, :, :, others], r0.at[two], swap_slots[m], sib)
+
     known = pltpu.make_async_copy(table, offs_all, here.at[8])
     known.start()
     visit_positions(amps.shape[0], offs, ext, whole_probe, amps, squares, turns, frame, sums,
-                    patch, far, fac, grad, mask)
+                    patch, far, fac, grad, mask, lambda m: swap(m).start())
     known.wait()
     spread = lax.broadcasted_iota(jnp.int32, (8, N), 1) - lax.broadcasted_iota(jnp.int32, (8, N), 0)
     lane = lax.broadcasted_iota(jnp.int32, (24, 128), 1)
@@ -429,7 +452,13 @@
         for k in range(half - 1, 0, -1):
             order += [k, -k]
         order += [0]
-        swaps = {k: w.start(frame.at[:, zat(k), 1 - c], s.at[zat(k)], w.slot(), sib) for k in order}
+        swaps = {}
+
+        def swap_more(count):
+            for k in order[len(swaps):len(swaps) + count]:
+                swaps[k] = w.start(frame.at[:, zat(k), 1 - c], s.at[zat(k)], w.slot(), sib)
+
+        swap_more(3)
         yield
 
         def mine(k):
@@ -451,6 +480,7 @@
                         s[d, parts[part]] += box[step - 1, parts[part]]
                     went[step, way, part] = w.start(
                         s.at[d, parts[part]], box.at[step, parts[part]], w.slot(), zdev(way))
+            swap_more(3)
             weigh(step)
             yield
         mine(0)
@@ -477,45 +507,64 @@
             wide[ch, :, :, 128:128 + TILE] = obj[ch] + acc[ch] / share
         h1 = w.start(wide.at[:, :, :, TILE:TILE + 128], hl, w.slot(), {"tx": right_})
         h2 = w.start(wide.at[:, :, :, 128:256], hr, w.slot(), {"tx": left})
+        for ch in range(2):
+            for g in range(3):
+                k = 3 * ch + g
+                tops[k:k + 1, :] = wide[ch, g, 0:1, 128:128 + TILE]
+                bots[k:k + 1, :] = wide[ch, g, 7:8, 128:128 + TILE]
+        inner, first, final = pl.ds(128, TILE), pl.ds(0, 128), pl.ds(128 + TILE, 128)
+        rows_sent = [
+            w.start(bots, up_in.at[:, inner], w.slot(), {"pos": following}),
+            w.start(tops, dn_in.at[:, inner], w.slot(), {"pos": previous}),
+            w.start(bots.at[:, 0:128], up_in.at[:, final], w.slot(), {"pos": following, "tx": left}),
+            w.start(tops.at[:, TILE - 128:TILE], dn_in.at[:, first], w.slot(), {"pos": previous, "tx": right_}),
+        ]
+        k3 = [w.slot(), w.slot()]
+        k4 = [w.slot(), w.slot()]
+
+        def last_down():
+            return [w.copy(bots, up_edge.at[:, inner], k3[0], {"pos": 0, "ty": down}),
+                    w.copy(bots.at[:, 0:128], up_edge.at[:, final], k3[1], {"pos": 0, "ty": down, "tx": left})]
+
+        def first_up():
+            return [w.copy(tops, dn_edge.at[:, inner], k4[0], {"pos": N_POS - 1, "ty": up}),
+                    w.copy(tops.at[:, TILE - 128:TILE], dn_edge.at[:, first], k4[1],
+                           {"pos": N_POS - 1, "ty": up, "tx": right_})]
+
+        @pl.when(p == N_POS - 1)
+        def _():
+            for made in last_down():
+                made.start()
+
+        @pl.when(p == 0)
+        def _():
+            for made in first_up():
+                made.start()
+
         yield
         h1.wait_recv()
         wide[:, :, :, 0:128] = jnp.where(b > 0, hl[...], 0.0)
         h2.wait_recv()
         wide[:, :, :, 128 + TILE:] = jnp.where(b < N_X - 1, hr[...], 0.0)
-        tops[...] = jnp.zeros_like(tops)
-        bots[...] = jnp.zeros_like(bots)
-        for ch in range(2):
-            for g in range(3):
-                k = 3 * ch + g
-                tops[k:k + 1, :] = wide[ch, g, 0:1, :]
-                bots[k:k + 1, :] = wide[ch, g, 7:8, :]
-        v1 = w.start(bots, up_in, w.slot(), {"pos": following})
-        v2 = w.start(tops, dn_in, w.slot(), {"pos": previous})
-        k3, k4 = w.slot(), w.slot()
+        for made in rows_sent:
+            made.wait_recv()
+
+        @pl.when(p == 0)
+        def _():
+            for made in last_down():
+                made.wait_recv()
+            for made in first_up():
+                made.wait_send()
 
         @pl.when(p == N_POS - 1)
         def _():
-            w.copy(bots, up_edge, k3, {"pos": 0, "ty": down}).start()
-
-        @pl.when(p == 0)
-        def _():
-            w.copy(tops, dn_edge, k4, {"pos": N_POS - 1, "ty": up}).start()
-
-        yield
-        v1.wait_recv()
-        v2.wait_recv()
-
-        @pl.when(p == 0)
-        def _():
-            made = w.copy(bots, up_edge, k3, {"pos": 0, "ty": down})
-            made.wait_recv()
-            w.copy(tops, dn_edge, k4, {"pos": N_POS - 1, "ty": up}).wait_send()
-
-        @pl.when(p == N_POS - 1)
-        def _():
-            w.copy(tops, dn_edge, k4, {"pos": N_POS - 1, "ty": up}).wait_recv()
-            w.copy(bots, up_edge, k3, {"pos": 0, "ty": down}).wait_send()
-
+            for made in first_up():
+                made.wait_recv()
+            for made in last_down():
+                made.wait_send()
+
+        in_left = lax.broadcasted_iota(jnp.int32, (1, EXT), 1) >= jnp.where(b > 0, 0, 128)
+        in_right = lax.broadcasted_iota(jnp.int32, (1, EXT), 1) < jnp.where(b < N_X - 1, EXT, 128 + TILE)
         sub = lax.broadcasted_iota(jnp.int32, (8, EXT), 0)
 
         def unit(x, below):
@@ -534,12 +583,12 @@
                     edge = jnp.where(a > 0, up_edge[3 * ch + 2:3 * ch + 3, :], 0.0)
                 else:
                     edge = up_in[k - 1:k, :]
-                first = jnp.where(p == 0, edge, up_in[k:k + 1, :])
+                first = jnp.where(in_right, jnp.where(p == 0, edge, up_in[k:k + 1, :]), 0.0)
                 if g == 2:
                     edge = jnp.where(a < N_Y - 1, dn_edge[3 * ch:3 * ch + 1, :], 0.0)
                 else:
                     edge = dn_in[k + 1:k + 2, :]
-                final = jnp.where(p == N_POS - 1, edge, dn_in[k:k + 1, :])
+                final = jnp.where(in_left, jnp.where(p == N_POS - 1, edge, dn_in[k:k + 1, :]), 0.0)
                 x.append(v)
                 above.append(jnp.where(sub == 0, first, pltpu.roll(v, 1, 0)))
                 below.append(jnp.where(sub == 7, final, pltpu.roll(v, 7, 0)))
@@ -586,9 +635,9 @@
         return lax.rem(b + (k + N_X), N_X)
 
     def probe_path():
-        swap = w.start(sums.at[:, :, :, :, :, others], r0, w.slot(), sib)
-        yield
-        swap.wait_recv()
+        for m in range(whole_probe.shape[0] + 1):
+            swap(m).wait_recv()
+            w.started.append(swap(m))
         r0[...] += sums[:, :, :, :, :, lanes]
         first = []
         for k in range(1, N_Y):
@@ -638,20 +687,23 @@
         yield
         for made in fifth:
             made.wait_recv()
-        sixth = []
+        sixth, pairs = [], []
         spot = pout.at[:, a, :, 0, :, lanes]
         for k in range(1, N_Y):
-            sixth.append(w.start(spot, spot, w.slot(), {"ty": at_y(k)}))
+            sixth.append((w.start(spot, spot, w.slot(), {"ty": at_y(k)}), pout.at[:, at_y(-k), :, 0, :, lanes]))
+        pairs.append(w.start(spot, spot, w.slot(), sib))
         spot = pout.at[:, :, b, 1, :, lanes]
         for k in range(1, N_X):
-            sixth.append(w.start(spot, spot, w.slot(), {"tx": at_x(k)}))
-        yield
-        for made in sixth:
-            made.wait_recv()
-        spot = pout.at[:, :, :, :, :, lanes]
-        last = w.start(spot, spot, w.slot(), sib)
-        yield
-        last.wait_recv()
+            sixth.append((w.start(spot, spot, w.slot(), {"tx": at_x(k)}), pout.at[:, :, at_x(-k), 1, :, lanes]))
+        pairs.append(w.start(spot, spot, w.slot(), sib))
+        yield
+        for k in (0, 3, 2, 5, 1, 4):
+            made, spot = sixth[k]
+            made.wait_recv()
+            pairs.append(w.start(spot, spot, w.slot(), sib))
+        yield
+        for made in pairs:
+            made.wait_recv()
         yield
 
     objects, probes = object_path(), probe_path()
@@ -663,8 +715,8 @@
     w.finish()
 
 
-MERGE_ORDER = "opo" + "po" + "opo" + "pop" + "opopo" + "oo"
-WIRES = 170
+MERGE_ORDER = "opooopopopoopopooopop"
+WIRES = 190
 
 
 def step_call(offs, obj, probe, amps, live):
@@ -698,7 +750,7 @@
             v(nz, g, 8, EXT), v(half, g, 8, EXT), v(half, g, 8, EXT), v(channels, 5, 8, EXT),
             v(channels, 3, 8, N), v(channels, 2, 8, TILE), v(channels, 2, 8, N), v(channels, 3, 8, TILE),
             v(2, 3, 8, EXT), v(2, 3, 8, 128), v(2, 3, 8, 128),
-            v(8, EXT), v(8, EXT), v(8, EXT), v(8, EXT), v(8, EXT), v(8, EXT),
+            v(8, TILE), v(8, TILE), v(8, EXT), v(8, EXT), v(8, EXT), v(8, EXT),
             v(9, N_Y, N_X, 2, 8, 128), v(2, 3, 9, 4, 8, 128), v(2, 9, 4, 8, 128), v(2, 3, 9, 8, 128),
             v(9, 2, 8, 128), v(8, 2, 2, 8, 128), v(7, 2, 2, 8, 128),
             pltpu.SemaphoreType.DMA((9,)), pltpu.SemaphoreType.DMA((WIRES,)), pltpu.SemaphoreType.DMA((WIRES,)),

time: 101 us -> 99.3 us (0.983)
  Pallas kernels: 96.9 us -> 94.7 us
    pallas_call x1, Pallas kernels: 96.9 us -> 94.7 us  [step_call(): pl.pallas_call(step_kernel, out_shape=(jax.ShapeDtypeStruct((2, 3, N_POS,...]
where the time goes in v3:
time: 99.3 us; the launch traced here: 99.2 us
  Pallas kernels  94.7 us (95%)
  local copies, waits for them, and re-layouts  3.83 us (4%)
    pallas_call x1, Pallas kernels, step_call(): pl.pallas_call(step_kernel, out_shape=(jax.ShapeDtypeStruct((2, 3, N_POS,...  94.7 us
    unnamed x4, local copies, waits for them, and re-layouts  3.83 us

profile of v3, /device:TPU:1, one launch (start us, length us, event | category | flops | bytes accessed | tf_op | source)
XLA Modules:
  0.0 99.2 jit_solution(10666927645504744955)
XLA Ops:
  0.6 94.7 %step.1 = (f32[2,3,16,8,384]{4,3,2,1,0:T(8,128)}, f32[8,4,4,2,8,256]{5,4,3,2,1,0:T(8,128)}) custom-call(s32[2,2]{1,0:T(2,128)} %offs.1, f32[2,3,16,8,384]{4,3,2,1,0:T(8,128)} %bitcast.7, f32[8,4,4,2,8,256]{5,4,3,2,1,0:T(8,128)} %bitcast.4, f32[2,256,256]{2,1,0:T(8,128)} %amps_far.1, s32[256,256]{1,0:T(8,128)} %live_far.1, ...), custom_call_target="tpu_custom_call" | custom-call | tf_op jit(solution)/shard_map/step/pallas_call | solution.py:735
  95.4 0.0 copy-start
  95.4 2.5 %copy.11 = f32[2,384,384]{2,1,0:T(8,128)} copy(f32[2,384,384]{2,1,0:T(8,128)} %bitcast.6) | data formatting | bytes 2359296
  97.9 0.0 copy-done
  97.9 1.3 %copy.12 = f32[4,2,256,256]{3,2,1,0:T(8,128)} copy(f32[4,2,256,256]{3,2,1,0:T(8,128)S(1)} %bitcast.5) | data formatting | bytes 4194304
Async XLA Ops:
  95.4 2.5 %copy-start = (f32[8,4,4,2,8,256]{5,4,3,2,1,0:T(8,128)S(1)}, f32[8,4,4,2,8,256]{5,4,3,2,1,0:T(8,128)}, u32[]{:S(2)}) copy-start(f32[8,4,4,2,8,256]{5,4,3,2,1,0:T(8,128)} %get-tuple-element.5) | copy-start | bytes 6291460

commit v4 on v3

--- a/solution.py
+++ b/solution.py
@@ -715,7 +715,7 @@
     w.finish()
 
 
-MERGE_ORDER = "opooopopopoopopooopop"
+MERGE_ORDER = "opoopoopopoopopooopop"
 WIRES = 190
 
 

time: 99.3 us -> 99.3 us (level)
  no operation moved by 1% of the time
where the time goes in v4:
time: 99.3 us; the launch traced here: 99.2 us
  Pallas kernels  94.7 us (95%)
  local copies, waits for them, and re-layouts  3.83 us (4%)
    pallas_call x1, Pallas kernels, step_call(): pl.pallas_call(step_kernel, out_shape=(jax.ShapeDtypeStruct((2, 3, N_POS,...  94.7 us
    unnamed x4, local copies, waits for them, and re-layouts  3.83 us

profile of v4, /device:TPU:1, one launch (start us, length us, event | category | flops | bytes accessed | tf_op | source)
XLA Modules:
  0.0 99.2 jit_solution(7443323802002246657)
XLA Ops:
  0.6 94.7 %step.1 = (f32[2,3,16,8,384]{4,3,2,1,0:T(8,128)}, f32[8,4,4,2,8,256]{5,4,3,2,1,0:T(8,128)}) custom-call(s32[2,2]{1,0:T(2,128)} %offs.1, f32[2,3,16,8,384]{4,3,2,1,0:T(8,128)} %bitcast.7, f32[8,4,4,2,8,256]{5,4,3,2,1,0:T(8,128)} %bitcast.4, f32[2,256,256]{2,1,0:T(8,128)} %amps_far.1, s32[256,256]{1,0:T(8,128)} %live_far.1, ...), custom_call_target="tpu_custom_call" | custom-call | tf_op jit(solution)/shard_map/step/pallas_call | solution.py:735
  95.4 0.0 copy-start
  95.4 2.5 %copy.11 = f32[2,384,384]{2,1,0:T(8,128)} copy(f32[2,384,384]{2,1,0:T(8,128)} %bitcast.6) | data formatting | bytes 2359296
  97.9 0.0 copy-done
  97.9 1.3 %copy.12 = f32[4,2,256,256]{3,2,1,0:T(8,128)} copy(f32[4,2,256,256]{3,2,1,0:T(8,128)S(1)} %bitcast.5) | data formatting | bytes 4194304
Async XLA Ops:
  95.4 2.5 %copy-start = (f32[8,4,4,2,8,256]{5,4,3,2,1,0:T(8,128)S(1)}, f32[8,4,4,2,8,256]{5,4,3,2,1,0:T(8,128)}, u32[]{:S(2)}) copy-start(f32[8,4,4,2,8,256]{5,4,3,2,1,0:T(8,128)} %get-tuple-element.5) | copy-start | bytes 6291460
